TPU v7x, 32 devices: a whole 2x2x4 slice. The times are simulated.
32 devices in a mesh: seq: 8 (over y, x, core), head: 4 (over z).
Axes of the slice: x: 2, y: 2, z: 4, core: 2. Of those that a mesh axis runs over, the one named last changes fastest.
Arguments:
- tokens: float32 [16384, 1024], P('seq'), may hold values from -6 to 6
- cotangent: float32 [16384, 1024], P('seq'), may hold values from -6 to 6
- sequence_starts: int32 [8], P('seq'), may hold values from 1 to 2048, as said below
- norm_gain: float32 [1024], replicated, may hold values from 0.5 to 1.5
- inner_weight: float32 [1024, 2, 2048], P('seq', None, 'head'), may hold values from -0.1875 to 0.1875
- state_weight: float32 [1024, 2, 128], P('seq', None, 'head'), may hold values from -0.1875 to 0.1875
- step_weight: float32 [1024, 32], P('seq', 'head'), may hold values from -0.1875 to 0.1875
- inner_params: float32 [6, 2048], P(None, 'head'), may hold values from -5 to 5
- state_conv: float32 [5, 2, 128], P(None, None, 'head'), may hold values from -3 to 3
- head_params: float32 [3, 32], P(None, 'head'), may hold values from -16 to 6
- output_weight: float32 [2048, 1024], P('head', 'seq'), may hold values from -0.125 to 0.125
- first_norm_gain: float32 [1024], replicated, may hold values from -768 to 768
- second_norm_gain: float32 [1024], replicated, may hold values from 16384 to 65536
- first_inner_weight: float32 [1024, 2, 2048], P('seq', None, 'head'), may hold values from -384 to 384
- second_inner_weight: float32 [1024, 2, 2048], P('seq', None, 'head'), may hold values from 4096 to 16384
- first_state_weight: float32 [1024, 2, 128], P('seq', None, 'head'), may hold values from -384 to 384
- second_state_weight: float32 [1024, 2, 128], P('seq', None, 'head'), may hold values from 4096 to 16384
- first_step_weight: float32 [1024, 32], P('seq', 'head'), may hold values from -384 to 384
- second_step_weight: float32 [1024, 32], P('seq', 'head'), may hold values from 4096 to 16384
- first_inner_params: float32 [6, 2048], P(None, 'head'), may hold values from -768 to 768
- second_inner_params: float32 [6, 2048], P(None, 'head'), may hold values from 16384 to 65536
- first_state_conv: float32 [5, 2, 128], P(None, None, 'head'), may hold values from -768 to 768
- second_state_conv: float32 [5, 2, 128], P(None, None, 'head'), may hold values from 16384 to 65536
- first_head_params: float32 [3, 32], P(None, 'head'), may hold values from -3072 to 3072
- second_head_params: float32 [3, 32], P(None, 'head'), may hold values from 262144 to 1048576
- first_output_weight: float32 [2048, 1024], P('head', 'seq'), may hold values from -768 to 768
- second_output_weight: float32 [2048, 1024], P('head', 'seq'), may hold values from 16384 to 65536
Outputs:
- output: float32 [16384, 1024], P('seq')
- input_gradient: float32 [16384, 1024], P('seq')
- next_norm_gain: float32 [1024], replicated
- next_first_norm_gain: float32 [1024], replicated
- next_second_norm_gain: float32 [1024], replicated
- next_inner_weight: float32 [1024, 2, 2048], P('seq', None, 'head')
- next_first_inner_weight: float32 [1024, 2, 2048], P('seq', None, 'head')
- next_second_inner_weight: float32 [1024, 2, 2048], P('seq', None, 'head')
- next_state_weight: float32 [1024, 2, 128], P('seq', None, 'head')
- next_first_state_weight: float32 [1024, 2, 128], P('seq', None, 'head')
- next_second_state_weight: float32 [1024, 2, 128], P('seq', None, 'head')
- next_step_weight: float32 [1024, 32], P('seq', 'head')
- next_first_step_weight: float32 [1024, 32], P('seq', 'head')
- next_second_step_weight: float32 [1024, 32], P('seq', 'head')
- next_inner_params: float32 [6, 2048], P(None, 'head')
- next_first_inner_params: float32 [6, 2048], P(None, 'head')
- next_second_inner_params: float32 [6, 2048], P(None, 'head')
- next_state_conv: float32 [5, 2, 128], P(None, None, 'head')
- next_first_state_conv: float32 [5, 2, 128], P(None, None, 'head')
- next_second_state_conv: float32 [5, 2, 128], P(None, None, 'head')
- next_head_params: float32 [3, 32], P(None, 'head')
- next_first_head_params: float32 [3, 32], P(None, 'head')
- next_second_head_params: float32 [3, 32], P(None, 'head')
- next_output_weight: float32 [2048, 1024], P('head', 'seq')
- next_first_output_weight: float32 [2048, 1024], P('head', 'seq')
- next_second_output_weight: float32 [2048, 1024], P('head', 'seq')
Inputs may be any that keep to these rules, and one draw needn't show every extreme that they name: `sequence_starts`: entry k is the offset within the k-th block of 2048 tokens at which a new sequence begins, or 2048 where none begins there; the stream also begins a sequence at token 0. New sequences begin only in the first and the last block, so one sequence runs from the first block to the last.
All inputs are finite; a program needn't handle non-finite values.
Results may differ from a plain program's by a relative error of at most 0.0015.
The roundings to bfloat16 on the way count: a program that leaves them out, or rounds other values in their place, can miss the bound.
Values may be sent and summed in bfloat16 or wider, within the bound.
No kernel may reach another device: no remote copies, remote signals or barrier semaphores. Data moves between devices by JAX's collectives and lax.ppermute only.
A program may use at most 192 MiB of HBM per device.

v0:
```python
import jax
import jax.numpy as jnp
from jax import lax
from jax.sharding import PartitionSpec as P

D = 1024
HEADDIM = 64
STATE = 128
CONV = 4
BLOCK = 256
STEP = 10
INNER = 2048


norm_epsilon = 1e-05
adam_epsilon = 1e-08
moment_decay = 0.5
weight_decay = 0.1
highest = lax.Precision.HIGHEST


def passed_along(value, axis, steps):
    count = lax.axis_size(axis)
    first, last = (max(0, -steps), min(count, count - steps))
    return lax.ppermute(value, axis, [(source, source + steps) for source in range(first, last)])


def carried_in(part, axis, combine, identity, reverse):
    count = lax.axis_size(axis)
    place = lax.axis_index(axis)
    ahead = count - 1 - place if reverse else place
    gathered = jax.tree.map(lambda a: lax.all_gather(a, axis), part)
    state = jax.tree.map(lambda a, e: jnp.zeros_like(a) + jnp.asarray(e, a.dtype), part, identity)

    def one(step, state):
        source = count - 1 - step if reverse else step
        return combine(
            state, jax.tree.map(lambda a: lax.dynamic_index_in_dim(a, source, 0, False), gathered)
        )

    return lax.fori_loop(0, ahead, one, state)


def decay_terms(raw_steps, head_local):
    steps = jax.nn.softplus(raw_steps + head_local[0])
    return (steps, -jnp.exp(head_local[1]) * steps)


def block_view(array, count):
    return array.reshape((count, BLOCK) + array.shape[1:])


def entering_segments(blocked):
    return jnp.concatenate([jnp.zeros((1,), jnp.int32), blocked[:-1, -1]])


def block_states(values, raw_steps, head_local, keys, segments):
    count = values.shape[0] // BLOCK
    heads_local = head_local.shape[1]
    steps, logdecay = decay_terms(raw_steps, head_local)
    cumulative = jnp.cumsum(block_view(logdecay, count), axis=1)
    blocked = block_view(segments, count)
    ending = (blocked == blocked[:, -1:]).astype(jnp.float32)
    weights_end = (
        jnp.exp(cumulative[:, -1:, :] - cumulative) * ending[:, :, None] * block_view(steps, count)
    )
    shaped = block_view(values, count).reshape(count, BLOCK, heads_local, HEADDIM)
    states = jnp.einsum(
        "cjh,cjhp,cjn->chpn", weights_end, shaped, block_view(keys, count), precision=highest
    )
    keep_last = (blocked[:, -1] == entering_segments(blocked)).astype(jnp.float32)
    decays = jnp.exp(cumulative[:, -1, :]) * keep_last[:, None]
    return (states, decays)


def block_outputs(values, raw_steps, head_local, keys, queries, segments, entering):
    count = values.shape[0] // BLOCK
    heads_local = head_local.shape[1]
    steps, logdecay = decay_terms(raw_steps, head_local)
    cumulative = jnp.cumsum(block_view(logdecay, count), axis=1)
    blocked = block_view(segments, count)
    order = jnp.arange(BLOCK)
    same = (blocked[:, :, None] == blocked[:, None, :]) & (order[:, None] >= order[None, :])[None]
    spread = cumulative[:, :, None, :] - cumulative[:, None, :, :]
    decay = jnp.where(same[..., None], jnp.exp(jnp.where(same[..., None], spread, 0.0)), 0.0)
    blocked_queries = block_view(queries, count)
    scores = jnp.einsum("cin,cjn->cij", blocked_queries, block_view(keys, count), precision=highest)
    mixing = scores[..., None] * decay * block_view(steps, count)[:, None, :, :]
    shaped = block_view(values, count).reshape(count, BLOCK, heads_local, HEADDIM)
    inner = jnp.einsum("cijh,cjhp->cihp", mixing, shaped, precision=highest)
    keep = (blocked == entering_segments(blocked)[:, None]).astype(jnp.float32)
    carried = jnp.einsum("cin,chpn->cihp", blocked_queries, entering, precision=highest)
    carried = carried * (jnp.exp(cumulative) * keep[:, :, None])[..., None]
    mixed = inner + carried + head_local[2][None, None, :, None] * shaped
    return mixed.reshape(values.shape)


def conv_apply(extended, taps, segments):
    rows = segments.shape[0]
    padded_segments = jnp.concatenate([jnp.zeros((CONV - 1,), jnp.int32), segments])
    total = jnp.broadcast_to(taps[CONV], (rows, taps.shape[1]))
    for offset in range(CONV):
        match = (padded_segments[offset : offset + rows] == segments).astype(jnp.float32)
        total = total + taps[offset] * extended[offset : offset + rows] * match[:, None]
    return jax.nn.silu(total)


def chain_combine(earlier, later):
    return (earlier[0] * later[0], later[0][:, None, None] * earlier[1] + later[1])


def adamw(weight, gradient, first, second, rate, shrink):
    first_new = moment_decay * first + (1.0 - moment_decay) * gradient
    second_new = moment_decay * second + (1.0 - moment_decay) * gradient * gradient
    correction = 1.0 - moment_decay**STEP
    ratio = first_new / correction / (jnp.sqrt(second_new / correction) + adam_epsilon)
    return (weight - rate * (ratio + shrink * weight), first_new, second_new)


def on_device(
    tokens,
    cotangent,
    sequence_starts,
    norm_gain,
    inner_weight,
    state_weight,
    step_weight,
    inner_params,
    state_conv,
    head_params,
    output_weight,
    first_norm_gain,
    second_norm_gain,
    first_inner_weight,
    second_inner_weight,
    first_state_weight,
    second_state_weight,
    first_step_weight,
    second_step_weight,
    first_inner_params,
    second_inner_params,
    first_state_conv,
    second_state_conv,
    first_head_params,
    second_head_params,
    first_output_weight,
    second_output_weight,
):
    rows = tokens.shape[0]
    width = tokens.shape[1]
    inner_local = inner_weight.shape[2]
    state_local = state_weight.shape[2]
    heads_local = step_weight.shape[1]
    count = rows // BLOCK
    places = jnp.arange(rows, dtype=jnp.int32)
    segments = (places >= sequence_starts[0]).astype(jnp.int32)
    tail_keep = (segments[rows - CONV + 1 :] == segments[rows - 1]).astype(jnp.float32)
    inner_full, state_full, step_full, output_full = (
        lax.all_gather(inner_weight.astype(jnp.bfloat16), "seq", axis=0, tiled=True),
        lax.all_gather(state_weight.astype(jnp.bfloat16), "seq", axis=0, tiled=True),
        lax.all_gather(step_weight.astype(jnp.bfloat16), "seq", axis=0, tiled=True),
        lax.all_gather(output_weight.astype(jnp.bfloat16), "seq", axis=1, tiled=True),
    )
    input_matrix = jnp.concatenate(
        [
            inner_full.reshape(width, 2 * inner_local),
            state_full.reshape(width, 2 * state_local),
            step_full,
        ],
        axis=1,
    )
    split_two = 2 * inner_local
    split_three = split_two + 2 * state_local
    inverse = lax.rsqrt(jnp.mean(tokens * tokens, axis=1, keepdims=True) + norm_epsilon)
    rounded = (tokens * inverse * norm_gain).astype(jnp.bfloat16)
    projected = jnp.dot(rounded, input_matrix, preferred_element_type=jnp.float32)
    gates = projected[:, :inner_local]
    conv_in = projected[:, inner_local:split_three].astype(jnp.bfloat16)
    raw_steps = projected[:, split_three:]
    tail = conv_in[rows - CONV + 1 :] * tail_keep[:, None].astype(jnp.bfloat16)
    before = passed_along(tail, "seq", 1)
    extended = jnp.concatenate([before, conv_in], axis=0).astype(jnp.float32)
    taps = jnp.concatenate(
        [inner_params[: CONV + 1], state_conv.reshape(CONV + 1, 2 * state_local)], axis=1
    )
    activated, conv_pullback = jax.vjp(
        lambda ext, tap: conv_apply(ext, tap, segments), extended, taps
    )
    values = activated[:, :inner_local]
    keys_local = activated[:, inner_local:].astype(jnp.bfloat16).reshape(rows, 2, state_local)
    keys_queries = lax.all_gather(keys_local, "head", axis=2, tiled=True).astype(jnp.float32)
    keys = keys_queries[:, 0]
    queries = keys_queries[:, 1]
    (states, decays), state_pullback = jax.vjp(
        lambda val, raw, hed, key_in: block_states(val, raw, hed, key_in, segments),
        values,
        raw_steps,
        head_params,
        keys,
    )
    device_decay = jnp.ones((heads_local,), jnp.float32)
    device_state = jnp.zeros((heads_local, HEADDIM, STATE), jnp.float32)
    for block in range(count):
        device_state = decays[block][:, None, None] * device_state + states[block]
        device_decay = device_decay * decays[block]
    identity = (
        jnp.ones((heads_local,), jnp.float32),
        jnp.zeros((heads_local, HEADDIM, STATE), jnp.float32),
    )
    incoming = carried_in((device_decay, device_state), "seq", chain_combine, identity, False)[1]
    entering_list = []
    current = incoming
    for block in range(count):
        entering_list.append(current)
        current = decays[block][:, None, None] * current + states[block]
    entering = jnp.stack(entering_list)
    mixed, output_pullback = jax.vjp(
        lambda val, raw, hed, key_in, query_in, enter: block_outputs(
            val, raw, hed, key_in, query_in, segments, enter
        ),
        values,
        raw_steps,
        head_params,
        keys,
        queries,
        entering,
    )
    silu_gates = jax.nn.silu(gates)
    gated = mixed * silu_gates
    squares = lax.psum(jnp.sum(gated * gated, axis=1), "head")
    gate_scale = lax.rsqrt(squares / INNER + norm_epsilon)
    gate_gain = inner_params[CONV + 1]
    unit = gated * gate_scale[:, None]
    gate_out = (unit * gate_gain).astype(jnp.bfloat16)
    partial_out = jnp.dot(gate_out, output_full, preferred_element_type=jnp.float32)
    output = tokens + lax.psum(partial_out, "head")
    back_round = cotangent.astype(jnp.bfloat16)
    gate_out_grad = lax.dot_general(
        back_round, output_full, (((1,), (1,)), ((), ())), preferred_element_type=jnp.float32
    )
    output_weight_grad = lax.dot_general(
        gate_out, back_round, (((0,), (0,)), ((), ())), preferred_element_type=jnp.float32
    )
    gain_grad = jnp.sum(gate_out_grad * unit, axis=0)
    unit_grad = gate_out_grad * gate_gain
    scale_part = jnp.sum(unit_grad * gated, axis=1) * -0.5 * gate_scale**3 / INNER
    squares_grad = lax.psum(scale_part, "head")
    gated_grad = unit_grad * gate_scale[:, None] + 2.0 * gated * squares_grad[:, None]
    mixed_grad = gated_grad * silu_gates
    sigmoid_gates = jax.nn.sigmoid(gates)
    gates_grad = gated_grad * mixed * sigmoid_gates * (1.0 + gates * (1.0 - sigmoid_gates))
    values_grad, steps_grad, head_grad, keys_grad, queries_grad, entering_grad = output_pullback(
        mixed_grad
    )
    local_grad = jnp.zeros((heads_local, HEADDIM, STATE), jnp.float32)
    for block in reversed(range(count)):
        local_grad = entering_grad[block] + decays[block][:, None, None] * local_grad
    outgoing = carried_in((device_decay, local_grad), "seq", chain_combine, identity, True)[1]
    state_grads = []
    decay_grads = []
    flowing = outgoing
    for block in reversed(range(count)):
        state_grads.insert(0, flowing)
        decay_grads.insert(0, jnp.sum(flowing * entering[block], axis=(1, 2)))
        flowing = entering_grad[block] + decays[block][:, None, None] * flowing
    values_more, steps_more, head_more, keys_more = state_pullback(
        (jnp.stack(state_grads), jnp.stack(decay_grads))
    )
    values_grad = values_grad + values_more
    steps_grad = steps_grad + steps_more
    head_total = head_grad + head_more
    key_query_grad = jnp.stack([keys_grad + keys_more, queries_grad], axis=1)
    local_key_grad = lax.psum_scatter(key_query_grad, "head", scatter_dimension=2, tiled=True)
    activated_grad = jnp.concatenate(
        [values_grad, local_key_grad.reshape(rows, 2 * state_local)], axis=1
    )
    extended_grad, taps_grad = conv_pullback(activated_grad)
    returned = passed_along(extended_grad[: CONV - 1], "seq", -1)
    conv_in_grad = extended_grad[CONV - 1 :]
    conv_in_grad = conv_in_grad.at[rows - CONV + 1 :].add(returned * tail_keep[:, None])
    projected_grad = jnp.concatenate([gates_grad, conv_in_grad, steps_grad], axis=1).astype(
        jnp.bfloat16
    )
    normed_part = lax.dot_general(
        projected_grad, input_matrix, (((1,), (1,)), ((), ())), preferred_element_type=jnp.float32
    )
    matrix_grad = lax.dot_general(
        rounded, projected_grad, (((0,), (0,)), ((), ())), preferred_element_type=jnp.float32
    )
    normed_grad = lax.psum(normed_part, "head")
    scaled_grad = normed_grad * norm_gain
    norm_gain_grad = jnp.sum(normed_grad * tokens * inverse, axis=0)
    input_gradient = (
        cotangent
        + inverse * scaled_grad
        - tokens * inverse**3 * jnp.mean(scaled_grad * tokens, axis=1, keepdims=True)
    )
    inner_total, state_total, step_total, output_total = (
        lax.psum_scatter(
            matrix_grad[:, :split_two].reshape(width, 2, inner_local),
            "seq",
            scatter_dimension=0,
            tiled=True,
        ),
        lax.psum_scatter(
            matrix_grad[:, split_two:split_three].reshape(width, 2, state_local),
            "seq",
            scatter_dimension=0,
            tiled=True,
        ),
        lax.psum_scatter(matrix_grad[:, split_three:], "seq", scatter_dimension=0, tiled=True),
        lax.psum_scatter(output_weight_grad, "seq", scatter_dimension=1, tiled=True),
    )
    params_local = jnp.concatenate([taps_grad[:, :inner_local], gain_grad[None]], axis=0)
    conv_local = taps_grad[:, inner_local:].reshape(CONV + 1, 2, state_local)
    gain_total, params_total, conv_total, head_sum = lax.psum(
        (norm_gain_grad, params_local, conv_local, head_total), "seq"
    )
    matrix_rate = 2.0 * D ** (-0.5)
    output_rate = 2.0 * INNER ** (-0.5)
    gain_next = adamw(norm_gain, gain_total, first_norm_gain, second_norm_gain, 0.5, 0.0)
    inner_next = adamw(
        inner_weight,
        inner_total,
        first_inner_weight,
        second_inner_weight,
        matrix_rate,
        weight_decay,
    )
    state_next = adamw(
        state_weight,
        state_total,
        first_state_weight,
        second_state_weight,
        matrix_rate,
        weight_decay,
    )
    step_next = adamw(
        step_weight, step_total, first_step_weight, second_step_weight, matrix_rate, weight_decay
    )
    params_next = adamw(
        inner_params, params_total, first_inner_params, second_inner_params, 0.5, 0.0
    )
    conv_next = adamw(state_conv, conv_total, first_state_conv, second_state_conv, 0.5, 0.0)
    head_next = adamw(head_params, head_sum, first_head_params, second_head_params, 3.0, 0.0)
    output_next = adamw(
        output_weight,
        output_total,
        first_output_weight,
        second_output_weight,
        output_rate,
        weight_decay,
    )
    return (
        output,
        input_gradient,
        gain_next[0],
        gain_next[1],
        gain_next[2],
        inner_next[0],
        inner_next[1],
        inner_next[2],
        state_next[0],
        state_next[1],
        state_next[2],
        step_next[0],
        step_next[1],
        step_next[2],
        params_next[0],
        params_next[1],
        params_next[2],
        conv_next[0],
        conv_next[1],
        conv_next[2],
        head_next[0],
        head_next[1],
        head_next[2],
        output_next[0],
        output_next[1],
        output_next[2],
    )


def solution(mesh):
    placed = (
        P("seq", None),
        P("seq", None),
        P("seq"),
        P(),
        P("seq", None, "head"),
        P("seq", None, "head"),
        P("seq", "head"),
        P(None, "head"),
        P(None, None, "head"),
        P(None, "head"),
        P("head", "seq"),
        P(),
        P(),
        P("seq", None, "head"),
        P("seq", None, "head"),
        P("seq", None, "head"),
        P("seq", None, "head"),
        P("seq", "head"),
        P("seq", "head"),
        P(None, "head"),
        P(None, "head"),
        P(None, None, "head"),
        P(None, None, "head"),
        P(None, "head"),
        P(None, "head"),
        P("head", "seq"),
        P("head", "seq"),
    )
    return jax.shard_map(
        on_device,
        mesh=mesh,
        in_specs=placed,
        out_specs=(
            P("seq", None),
            P("seq", None),
            P(),
            P(),
            P(),
            P("seq", None, "head"),
            P("seq", None, "head"),
            P("seq", None, "head"),
            P("seq", None, "head"),
            P("seq", None, "head"),
            P("seq", None, "head"),
            P("seq", "head"),
            P("seq", "head"),
            P("seq", "head"),
            P(None, "head"),
            P(None, "head"),
            P(None, "head"),
            P(None, None, "head"),
            P(None, None, "head"),
            P(None, None, "head"),
            P(None, "head"),
            P(None, "head"),
            P(None, "head"),
            P("head", "seq"),
            P("head", "seq"),
            P("head", "seq"),
        ),
        check_vma=False,
    )
```

profile of v0, /device:TPU:0, one launch (start us, length us, event | category | flops | bytes accessed | tf_op | source)
XLA Modules:
  0.0 1319.7 jit_solution(12466164446548596675)
XLA Ops:
  10.0 10.5 all_gather.30
  21.4 8.9 all_gather.31
  48.2 8.5 fusion.119
  88.4 16.0 %all-gather.9.cloned.1.call-done = bf16[2048,2,128]{0,2,1:T(8,128)(2,1)} async-done(((bf16[2048,2,32]{0,2,1:T(8,128)(2,1)}), bf16[2048,2,128]{0,2,1:T(8,128)(2,1)}) %all-gather.9.cloned.1.call-update) | async-done | bytes 1048592 | tf_op jit(solution)/shard_map/all_gather | solution.py:191
  119.5 9.7 all-gather
  134.2 8.1 all-gather.11.cloned.1.call-done
  150.3 21.3 %fusion.29 = f32[8,256,8,64]{1,3,2,0:T(8,128)S(1)} fusion(f32[8,256,8,64]{1,3,2,0:T(8,128)S(1)} %fusion.121, f32[8,256,8,64]{1,0,3,2:T(8,128)S(1)} %bitcast.321, f32[8,256,8]{1,2,0:T(8,128)S(1)} %bitcast.360, f32[8,256,8]{1,2,0:T(8,128)S(1)} %copy-done.72, f32[8,256,256]{2,1,0:T(8,128)S(1)} %copy-done.41, pred[8,256,256]{2,1,0:T(8,128)(4,1)S(1)} %copy-done.52, ...), kind=kOutput, calls=%fused_computation.56 | convolution fusion | flops 3246391296 | bytes 15400992 | tf_op jit(solution)/shard_map/jvp(cijh,cjhp->cihp)/dot_general | solution.py:90
  183.1 11.8 psum.56
  195.0 8.4 fusion.55
  203.5 49.2 %reduce-scatter.11.cloned.1.call-done = f32[512,128]{1,0:T(8,128)} async-done(((f32[512,1024]{1,0:T(8,128)}), f32[512,128]{1,0:T(8,128)}) %reduce-scatter.11.cloned.1.call-update) | async-done | bytes 262160 | tf_op jit(solution)/shard_map/reduce_scatter | solution.py:312
  254.7 23.7 %all-gather.13.cloned.1.call-done = bf16[512,1024]{1,0:T(8,128)(2,1)} async-done(((bf16[512,128]{1,0:T(8,128)(2,1)}), bf16[512,1024]{1,0:T(8,128)(2,1)}) %all-gather.13.cloned.1.call-update) | async-done | bytes 1048592 | tf_op jit(solution)/shard_map/all_gather | solution.py:162
  278.4 10.1 multiply_reduce_fusion.10
  288.5 11.8 psum.58
  300.4 11.1 multiply_reduce_fusion.9
  316.6 8.5 fusion.68
  326.2 34.1 %fusion.9 = (f32[8,256,8]{1,2,0:T(8,128)}, f32[8,256,8]{1,2,0:T(8,128)}, f32[8,256,8]{1,2,0:T(8,128)}, f32[8,256,256]{2,1,0:T(8,128)S(1)}) fusion(f32[8,256,8]{1,2,0:T(8,128)} %bitcast.358, f32[8,256,8]{1,2,0:T(8,128)} %get-tuple-element.302, f32[8,256,256]{2,1,0:T(8,128)} %fusion.120, pred[8,256,256]{2,1,0:T(8,128)(4,1)} %compare_and_fusion, ...), kind=kOutput, calls=%fused_computation.16 | convolution fusion | flops 3283566592 | bytes 13434880 | tf_op jit(solution)/shard_map/transpose(jvp(cijh,cjhp->cihp))/dot_general | solution.py:90
  382.6 21.1 %reduce-window.24 = f32[8,8,2,128]{3,1,2,0:T(8,128)} reduce-window(f32[8,8,2,128]{3,1,2,0:T(8,128)} %copy.419, f32[]{:T(128)} %constant.176.clone.1), window={size=1x1x1x128 pad=0_0x0_0x0_0x0_127}, to_apply=%region_18.20 | reduce-window | flops 2080768 | bytes 131076 | tf_op jit(solution)/shard_map/reduce-window.2
  408.3 17.9 %while.28 = (s32[]{:T(128)}, f32[8,64,128]{2,1,0:T(8,128)}, s32[]{:T(128)}, f32[8,8]{1,0:T(8,128)}, f32[8,8,64,128]{3,2,1,0:T(8,128)}, /*index=5*/s32[]{:T(128)}, s32[]{:T(128)}, s32[]{:T(128)}, s32[]{:T(128)}) while((s32[]{:T(128)}, f32[8,64,128]{2,1,0:T(8,128)}, s32[]{:T(128)}, f32[8,8]{1,0:T(8,128)}, f32[8,8,64,128]{3,2,1,0:T(8,128)}, ...), condition=%wide.region_11.13_spmd, body=%wide.region_10.12_spmd.sunk | while | flops 131078 | bytes 786675 | solution.py:41
  435.5 7.4 fusion.65
  455.2 17.7 %fusion.25 = f32[8,256,8,64]{1,3,2,0:T(8,128)S(1)} fusion(f32[8,256,8,64]{1,3,2,0:T(8,128)S(1)} %fusion.122, f32[8,256,8,64]{1,0,3,2:T(8,128)S(1)} %bitcast.328, f32[8,256,8]{1,2,0:T(8,128)S(1)} %bitcast.361, f32[8,256,8]{1,2,0:T(8,128)S(1)} %copy-done.73, f32[8,256,256]{2,1,0:T(8,128)S(1)} %copy-done.42, pred[8,256,256]{2,1,0:T(8,128)(4,1)S(1)} %copy-done.53, ...), kind=kOutput, calls=%fused_computation.51 | convolution fusion | flops 3246391296 | bytes 15400992 | tf_op jit(solution)/shard_map/transpose(jvp(cijh,cjhp->cihp))/dot_general | solution.py:90
  485.5 19.8 %reduce-window.26 = f32[8,8,2,128]{3,1,2,0:T(8,128)S(1)} reduce-window(f32[8,8,2,128]{3,1,2,0:T(8,128)S(1)} %copy.432, f32[]{:T(128)} %constant.176.clone.1), window={size=1x1x1x128 pad=0_0x0_0x0_0x0_127}, to_apply=%region_29.31 | reduce-window | flops 2080768 | bytes 131076 | tf_op jit(solution)/shard_map/reduce-window.4
  507.3 12.9 multiply_reduce_fusion.7
  531.4 10.3 fusion.63
  551.0 7.2 copy.435
  559.5 8.2 fusion.101
  567.7 8.2 fusion.64
  579.5 30.7 %reduce-scatter.7.cloned.1.call-done = f32[128,2,32]{0,2,1:T(8,128)} async-done(((f32[1024,2,32]{0,2,1:T(8,128)}), f32[128,2,32]{0,2,1:T(8,128)}) %reduce-scatter.7.cloned.1.call-update) | async-done | bytes 32784 | tf_op jit(solution)/shard_map/reduce_scatter | solution.py:305
  611.7 82.7 %all-reduce.23.cloned.1.call-done = f32[1024,2,512]{2,1,0:T(2,128)} async-done(((f32[1024,2,512]{2,1,0:T(2,128)}), f32[1024,2,512]{2,1,0:T(2,128)}) %all-reduce.23.cloned.1.call-update) | async-done | bytes 4194320
  698.2 563.0 %all-reduce.25.cloned.1.call-done = (f32[2048,1024]{1,0:T(8,128)}, f32[2048,1024]{1,0:T(8,128)}) async-done(((f32[2048,1024]{1,0:T(8,128)}, f32[2048,1024]{1,0:T(8,128)}), (f32[2048,1024]{1,0:T(8,128)}, f32[2048,1024]{1,0:T(8,128)})) %all-reduce.25.cloned.1.call-update) | async-done | bytes 16777232 | tf_op jit(solution)/shard_map/psum | solution.py:236
  1261.3 7.0 multiply_reduce_fusion.1
  1268.2 24.0 %all-reduce.18 = (f32[1024]{0:T(1024)S(1)}, f32[6,512]{1,0:T(8,128)S(1)}, f32[5,2,32]{2,1,0:T(2,128)S(1)}, f32[3,8]{1,0:T(4,128)S(1)}) all-reduce(f32[1024]{0:T(1024)S(1)} %get-tuple-element.176, f32[6,512]{1,0:T(8,128)S(1)} %pad_maximum_fusion.5, f32[5,2,32]{2,1,0:T(2,128)S(1)} %reshape.552, ...), channel_id=1, replica_groups=mesh['seq'=8,'head'=4] {'seq'}, use_global_device_ids=true, to_apply=%region_34.36 | all-reduce | flops 4440 | bytes 35520 | tf_op jit(solution)/shard_map/psum | solution.py:316
  1294.8 18.1 %multiply_subtract_fusion = (f32[2048,1024]{1,0:T(8,128)}, f32[2048,1024]{1,0:T(8,128)}) fusion(f32[2048,1024]{1,0:T(8,128)} %param.34, f32[2048,1024]{1,0:T(8,128)} %param.35, f32[2048,1024]{1,0:T(8,128)} %get-tuple-element.221, f32[2048]{0:T(1024)S(1)} %broadcast_multiply_fusion.4, f32[2048]{0:T(1024)S(1)} %copy-done.87, f32[1024]{0:T(1024)S(1)} %copy-done.76, ...), kind=kLoop, calls=%fused_computation.18 | loop fusion | flops 14680064 | bytes 50360320 | tf_op jit(solution)/shard_map/sub | solution.py:294
  (482 shorter events, 211.9 us)
Async XLA Ops:
  7.2 35.7 %all-gather.7.cloned.1.call-start = ((), (), s32[]{:S(2)}) async-start(), calls=%async_computation.4 | async-start | bytes 2359296 | tf_op jit(solution)/shard_map/all_gather | solution.py:159
  9.2 95.3 %all-gather.9.cloned.1.call-start = ((), (), s32[]{:S(2)}) async-start(), calls=%async_computation.5 | async-start | bytes 1310720 | tf_op jit(solution)/shard_map/all_gather | solution.py:191
  34.9 32.5 %copy-start.79 = (f32[576]{0:T(1024)}, f32[576]{0:T(1024)S(1)}, u32[]{:S(2)}) copy-start(f32[576]{0:T(1024)S(1)} %get-tuple-element.192) | copy-start | bytes 6916
  34.9 32.5 %copy-start.81 = (f32[576]{0:T(1024)}, f32[576]{0:T(1024)S(1)}, u32[]{:S(2)}) copy-start(f32[576]{0:T(1024)S(1)} %get-tuple-element.193) | copy-start | bytes 6916
  34.9 32.5 %copy-start.83 = (f32[576]{0:T(1024)}, f32[576]{0:T(1024)S(1)}, u32[]{:S(2)}) copy-start(f32[576]{0:T(1024)S(1)} %get-tuple-element.194) | copy-start | bytes 6916
  34.9 32.5 %copy-start.85 = (f32[576]{0:T(1024)}, f32[576]{0:T(1024)S(1)}, u32[]{:S(2)}) copy-start(f32[576]{0:T(1024)S(1)} %get-tuple-element.195) | copy-start | bytes 6916
  56.9 9.2 collective-permute-start
  76.1 66.2 %all-gather.11.cloned.1.call-start = ((), (), s32[]{:S(2)}) async-start(), calls=%async_computation.6 | async-start | bytes 2359296 | tf_op jit(solution)/shard_map/all_gather | solution.py:32
  112.9 33.2 %copy-start.8 = (f32[8,8,64,128]{3,2,1,0:T(8,128)}, f32[8,8,64,128]{3,2,1,0:T(8,128)S(1)}, u32[]{:S(2)}) copy-start(f32[8,8,64,128]{3,2,1,0:T(8,128)S(1)} %fusion.37) | copy-start | bytes 6291460
  114.7 137.9 %reduce-scatter.11.cloned.1.call-start = ((), (), s32[]{:S(2)}) async-start(), calls=%async_computation.12 | async-start | bytes 2359296 | tf_op jit(solution)/shard_map/reduce_scatter | solution.py:312
  195.0 57.7 %copy-start.56 = (f32[512,128]{1,0:T(8,128)S(1)}, f32[512,128]{1,0:T(8,128)}, u32[]{:S(2)}) copy-start(f32[512,128]{1,0:T(8,128)} %param.44) | copy-start | bytes 786436
  195.0 57.7 %copy-start.57 = (f32[512,128]{1,0:T(8,128)S(1)}, f32[512,128]{1,0:T(8,128)}, u32[]{:S(2)}) copy-start(f32[512,128]{1,0:T(8,128)} %param.59) | copy-start | bytes 786436
  195.0 57.6 %copy-start.58 = (f32[512,128]{1,0:T(8,128)S(1)}, f32[512,128]{1,0:T(8,128)}, u32[]{:S(2)}) copy-start(f32[512,128]{1,0:T(8,128)} %param.60) | copy-start | bytes 786436
  203.4 75.0 %all-gather.13.cloned.1.call-start = ((), (), s32[]{:S(2)}) async-start(), calls=%async_computation.7 | async-start | bytes 1179648 | tf_op jit(solution)/shard_map/all_gather | solution.py:162
  254.7 152.9 %all-gather.15.cloned.1.call-start = ((), (), s32[]{:S(2)}) async-start(), calls=%async_computation.8 | async-start | bytes 2359296 | tf_op jit(solution)/shard_map/all_gather | solution.py:32
  326.1 181.1 %reduce-scatter.5.cloned.1.call-start = ((), (), s32[]{:S(2)}) async-start(), calls=%async_computation.9 | async-start | bytes 2621440 | tf_op jit(solution)/shard_map/reduce_scatter | solution.py:273
  326.2 34.2 %copy-start.11 = (bf16[2048,1,128]{2,0,1:T(8,128)(2,1)S(1)}, bf16[2048,1,128]{2,0,1:T(8,128)(2,1)}, u32[]{:S(2)}) copy-start(bf16[2048,1,128]{2,0,1:T(8,128)(2,1)} %copy.390) | copy-start | bytes 1572868
  326.2 34.2 %copy-start.26 = (f32[8,256,128]{2,1,0:T(8,128)S(1)}, f32[8,256,128]{2,1,0:T(8,128)}, u32[]{:S(2)}) copy-start(f32[8,256,128]{2,1,0:T(8,128)} %fusion.68) | copy-start | bytes 3145732
  451.1 127.2 %reduce-scatter.9.cloned.1.call-start = ((), (), s32[]{:S(2)}) async-start(), calls=%async_computation.11 | async-start | bytes 36864 | tf_op jit(solution)/shard_map/reduce_scatter | solution.py:311
  522.1 6.9 collective-permute-start.1
  544.4 65.9 %reduce-scatter.7.cloned.1.call-start = ((), (), s32[]{:S(2)}) async-start(), calls=%async_computation.10 | async-start | bytes 294912 | tf_op jit(solution)/shard_map/reduce_scatter | solution.py:305
  546.1 148.3 %all-reduce.23.cloned.1.call-start = ((), (), s32[]{:S(2)}) async-start(), calls=%async_computation.13 | async-start | bytes 8388608
  558.3 702.9 %all-reduce.25.cloned.1.call-start = ((), (), s32[]{:S(2)}) async-start(), calls=%async_computation.14 | async-start | bytes 33554432 | tf_op jit(solution)/shard_map/psum | solution.py:236
  575.9 34.3 %copy-start.60 = (f32[128,2,32]{0,2,1:T(8,128)S(1)}, f32[128,2,32]{0,2,1:T(8,128)}, u32[]{:S(2)}) copy-start(f32[128,2,32]{0,2,1:T(8,128)} %param.39) | copy-start | bytes 98308
  575.9 34.3 %copy-start.88 = (f32[128,2,32]{0,2,1:T(8,128)S(1)}, f32[128,2,32]{0,2,1:T(8,128)}, u32[]{:S(2)}) copy-start(f32[128,2,32]{0,2,1:T(8,128)} %param.49) | copy-start | bytes 98308
  575.9 34.3 %copy-start.89 = (f32[128,2,32]{0,2,1:T(8,128)S(1)}, f32[128,2,32]{0,2,1:T(8,128)}, u32[]{:S(2)}) copy-start(f32[128,2,32]{0,2,1:T(8,128)} %param.50) | copy-start | bytes 98308
  575.9 118.5 %copy-start.43 = (f32[128,2,512]{2,1,0:T(2,128)S(1)}, f32[128,2,512]{2,1,0:T(2,128)}, u32[]{:S(2)}) copy-start(f32[128,2,512]{2,1,0:T(2,128)} %param.38) | copy-start | bytes 1572868
  576.0 118.4 %copy-start.54 = (f32[128,2,512]{2,1,0:T(2,128)S(1)}, f32[128,2,512]{2,1,0:T(2,128)}, u32[]{:S(2)}) copy-start(f32[128,2,512]{2,1,0:T(2,128)} %param.47) | copy-start | bytes 1572868
  576.0 118.4 %copy-start.55 = (f32[128,2,512]{2,1,0:T(2,128)S(1)}, f32[128,2,512]{2,1,0:T(2,128)}, u32[]{:S(2)}) copy-start(f32[128,2,512]{2,1,0:T(2,128)} %param.48) | copy-start | bytes 1572868
  1261.2 33.0 %copy-start.133 = (f32[3,8]{1,0:T(4,128)S(1)}, f32[3,8]{1,0:T(4,128)}, u32[]{:S(2)}) copy-start(f32[3,8]{1,0:T(4,128)} %param.57) | copy-start | bytes 292
  1261.2 32.9 %copy-start.134 = (f32[3,8]{1,0:T(4,128)S(1)}, f32[3,8]{1,0:T(4,128)}, u32[]{:S(2)}) copy-start(f32[3,8]{1,0:T(4,128)} %param.58) | copy-start | bytes 292
  1261.3 33.5 %copy-start.87 = (f32[2048]{0:T(1024)S(1)}, f32[2048]{0:T(1024)}, u32[]{:S(2)}) copy-start(f32[2048]{0:T(1024)} %get-tuple-element.304) | copy-start | bytes 24580
  (120 other events, 1071.6 us)
Sparse Core Ops, SparseCore 0:
  10.5 30.5 all-gather.6
  76.2 28.1 all-gather.8
  114.8 27.3 all-gather.10
  203.6 49.0 reduce-scatter.10
  254.8 23.5 all-gather.12
  326.2 25.1 all-gather.14
  451.2 39.7 reduce-scatter.4
  544.5 28.1 reduce-scatter.8
  576.6 33.5 reduce-scatter.6
  613.4 80.9 all-reduce.22
  697.8 563.3 all-reduce.24
where the time goes:
time: 1330 us; the launch traced here: 1320 us
  waiting for transfers between devices  774 us (58%)
  other arithmetic  191 us (14%)
  matrix products  165 us (12%)
  local copies, waits for them, and re-layouts  90.4 us (7%)
  blocking collectives  76.7 us (6%)
  between operations  17.5 us (1%)
    psum x1, waiting for transfers between devices, on_device(): output = tokens + lax.psum(partial_out, 'head')  563 us
    unnamed x12, waiting for transfers between devices  82.9 us
    dot_general x3, matrix products, block_outputs(): inner = jnp.einsum('cijh,cjhp->cihp', mixing, shaped, precision=highest)  73.1 us
    reduce_scatter x1, waiting for transfers between devices, on_device(): lax.psum_scatter(output_weight_grad, 'seq', scatter_dimension=1, tiled=True)  49.2 us
    another operation x10, other arithmetic  48.6 us
    reduce_scatter x1, waiting for transfers between devices, on_device(): lax.psum_scatter(matrix_grad[:, split_two:split_three].reshape(width, 2,...  30.7 us
  transfers between devices with their start and end apart: 13, of which 7 were waited for; matrix products, arithmetic and copies ran while one was open for 17% of the time, Pallas kernels for 0%

commit v1 on v0

v1 whole, which is shorter than its diff:
```python
import functools

import jax
import jax.numpy as jnp
from jax import lax
from jax.experimental import pallas as pl
from jax.experimental.pallas import tpu as pltpu
from jax.sharding import PartitionSpec as P

D = 1024
STATE = 128
CONV = 4
STEP = 10
INNER = 2048


norm_epsilon = 1e-05
adam_epsilon = 1e-08
moment_decay = 0.5
weight_decay = 0.1


def passed_along(value, axis, steps):
    count = lax.axis_size(axis)
    first, last = (max(0, -steps), min(count, count - steps))
    return lax.ppermute(value, axis, [(source, source + steps) for source in range(first, last)])


def carried_in(part, axis, reverse):
    count = lax.axis_size(axis)
    place = lax.axis_index(axis)
    parts = lax.all_gather(part, axis)
    states, decays = parts[:, :STATE], parts[:, STATE : STATE + 1]
    total = jnp.zeros_like(states[0])
    scale = jnp.ones_like(decays[0])
    for source in range(count) if reverse else reversed(range(count)):
        ahead = source > place if reverse else source < place
        total = total + jnp.where(ahead, scale, 0.0) * states[source]
        scale = scale * jnp.where(ahead, decays[source], 1.0)
    return total


def packed(block):
    top = jnp.max(jnp.abs(block), axis=0, keepdims=True)
    power = jnp.ceil(jnp.log2(jnp.maximum(top, 1e-30)))
    scaled = (block * jnp.exp2(14.0 - power)).astype(jnp.float16)
    note = jnp.broadcast_to(power, (16, block.shape[1])).astype(jnp.float16)
    return jnp.concatenate([scaled, note], axis=0)


def unpacked(message, zero=0.0):
    power = message[..., -16:-15, :].astype(jnp.float32) + zero
    return message[..., :-16, :].astype(jnp.float32) * jnp.exp2(power - 14.0)


def nothing(*others):
    total = jnp.float32(0.0)
    for other in others:
        first = lax.slice(other, (0,) * other.ndim, (1,) * other.ndim).reshape(())
        total = total + jnp.minimum(jnp.abs(first.astype(jnp.float32)), 0.0)
    return total


def halves_given(block, axis, bit):
    count = lax.axis_size(axis)
    upper = (lax.axis_index(axis) // bit) % 2
    half = block.shape[0] // 2
    kept = lax.dynamic_slice_in_dim(block, upper * half, half, 0)
    given = lax.dynamic_slice_in_dim(block, (1 - upper) * half, half, 0)
    pairs = [(place, place ^ bit) for place in range(count)]
    message = packed(given)
    return kept, message, lax.ppermute(message, axis, pairs)


def halves_joined(messages, axis, bit):
    count = lax.axis_size(axis)
    upper = (lax.axis_index(axis) // bit) % 2
    pairs = [(place, place ^ bit) for place in range(count)]
    other = lax.ppermute(messages, axis, pairs)
    return jnp.where(
        upper == 1,
        jnp.concatenate([other, messages], axis=0),
        jnp.concatenate([messages, other], axis=0),
    )


def halving_orders(axis):
    powers = [1 << power for power in range(lax.axis_size(axis).bit_length() - 1)]
    return powers, powers[::-1]


def reversed_bits(place, count):
    return sum((place // bit) % 2 * (count // (2 * bit)) for bit in halving_bits(count))


def halving_bits(count):
    return [1 << power for power in range(count.bit_length() - 1)]


class LineSum:
    def __init__(self, block, axis):
        self.axis = axis
        self.orders = halving_orders(axis)
        self.levels = len(self.orders[0])
        self.parts = list(jnp.split(block, 2))
        self.flight = None

    def send(self, level):
        sent = [
            halves_given(part, self.axis, order[level])
            for part, order in zip(self.parts, self.orders)
        ]
        self.parts = [kept for kept, _, _ in sent]
        self.sent = [message for _, message, _ in sent]
        self.flight = [arrived for _, _, arrived in sent]

    def receive(self, *others):
        zero = nothing(*others)
        self.parts = [
            part + unpacked(message, zero) for part, message in zip(self.parts, self.flight)
        ]

    def pack(self):
        self.parts = [packed(part)[None] for part in self.parts]

    def share(self, level):
        self.flight, self.sent = [], self.parts
        for part, order in zip(self.parts, self.orders):
            pairs = [(place, place ^ order[level]) for place in range(lax.axis_size(self.axis))]
            self.flight.append(lax.ppermute(part, self.axis, pairs))

    def join(self, level, *others):
        zero = nothing(*others)
        joined = []
        for part, other, order in zip(self.parts, self.flight, self.orders):
            upper = (lax.axis_index(self.axis) // order[level]) % 2
            joined.append(
                jnp.where(
                    upper.astype(jnp.float32) + zero > 0.5,
                    jnp.concatenate([other, part], axis=0),
                    jnp.concatenate([part, other], axis=0),
                )
            )
        self.parts = joined

    def result(self):
        return jnp.concatenate(
            [unpacked(part).reshape(-1, part.shape[-1]) for part in self.parts]
        )


CHUNK = 128
TILE = 256
LANES = 128
F32 = jnp.float32
BF16 = jnp.bfloat16


def mm(left, right, contract=((1,), (0,))):
    return lax.dot_general(left, right, (contract, ((), ())), preferred_element_type=F32)


NT = ((1,), (1,))
TN = ((0,), (0,))


def split(value):
    high = value.astype(BF16)
    return high, (value - high.astype(F32)).astype(BF16)


def split_three(value):
    high = value.astype(BF16)
    return (high,) + split(value - high.astype(F32))


def mm_exact(left, parts, contract=((1,), (0,))):
    return sum(mm(left, part, contract) for part in reversed(parts))


def mm_full(left, right, contract):
    pairs = ((1, 1), (2, 0), (0, 2), (1, 0), (0, 1), (0, 0))
    return sum(mm(left[i], right[j], contract) for i, j in pairs)


def logistic(value):
    return 1.0 / (1.0 + jnp.exp(-value))


def iota(shape, dim):
    return lax.broadcasted_iota(jnp.int32, shape, dim)


def triangle_sum(mask, value):
    return mm_exact(mask.astype(F32).astype(BF16), split_three(value))


def spread_pair(columns, pair):
    rows = columns.shape[0]
    first = jnp.broadcast_to(columns[:, 2 * pair : 2 * pair + 1], (rows, LANES))
    second = jnp.broadcast_to(columns[:, 2 * pair + 1 : 2 * pair + 2], (rows, LANES))
    return jnp.where(iota((rows, LANES), 1) < 64, first, second)


def spread_all(columns, width):
    return jnp.concatenate(
        [spread_pair(columns, pair) for pair in range(width // LANES)], axis=1
    )


def log_one_plus(value):
    ratio = value / (2.0 + value)
    square = ratio * ratio
    total = jnp.full_like(square, 1.0 / 15.0)
    for odd in (13, 11, 9, 7, 5, 3, 1):
        total = total * square + 1.0 / odd
    return 2.0 * ratio * total


def chunk_terms(raw, heads_row, begin, start):
    shifted = raw + heads_row[0:1]
    steps = jnp.maximum(shifted, 0.0) + log_one_plus(jnp.exp(-jnp.abs(shifted)))
    logdecay = -jnp.exp(heads_row[1:2]) * steps
    row = iota((CHUNK, CHUNK), 0)
    column = iota((CHUNK, CHUNK), 1)
    cumulative = triangle_sum(row >= column, logdecay)
    place = begin + iota((CHUNK, LANES), 0)
    segment = place >= start
    enter = begin - 1 >= start
    leave = begin + CHUNK - 1 >= start
    keep_in = jnp.where(segment == enter, 1.0, 0.0)
    keep_out = jnp.where(segment == leave, 1.0, 0.0)
    last = cumulative[CHUNK - 1 : CHUNK]
    entering = jnp.exp(cumulative) * keep_in
    leaving = jnp.exp(last - cumulative) * keep_out
    whole = jnp.exp(last) * jnp.where(enter == leave, 1.0, 0.0)
    return shifted, steps, logdecay, cumulative, entering, leaving, whole, segment


def forward_kernel(
    start_ref, rounded_ref, tail_ref, inner_ref, small_ref, taps_ref, heads_ref, gates_ref,
    pre_ref, conv_ref, kq_ref, raw_ref, local_ref, states_ref, reach_ref,
    factor_ref, final_ref, extended, state, offset,
):
    step = pl.program_id(0)
    width = gates_ref.shape[1]
    halo = tail_ref.shape[0]
    start = start_ref[0]
    low_lane = iota((CHUNK, LANES), 1) < 64

    def project(rounded):
        return mm(rounded, inner_ref[...]), mm(rounded, small_ref[...])

    @pl.when(step == 0)
    def _():
        state[...] = jnp.zeros_like(state)
        offset[...] = jnp.zeros_like(offset)
        wide, narrow = project(tail_ref[...])
        before = jnp.concatenate([wide[:, width:], narrow[:, : 2 * STATE]], axis=1)
        extended[0:halo] = before.astype(BF16).astype(F32)

    @pl.when(step > 0)
    def _():
        extended[0:halo] = extended[TILE : TILE + halo]

    wide, narrow = project(rounded_ref[...])
    gates_ref[...] = wide[:, :width]
    conv_in = jnp.concatenate([wide[:, width:], narrow[:, : 2 * STATE]], axis=1).astype(BF16)
    conv_ref[...] = conv_in
    raw_ref[...] = narrow[:, 2 * STATE :]
    extended[halo : halo + TILE] = conv_in.astype(F32)
    place = step * TILE + iota((TILE, 1), 0)
    pre = jnp.broadcast_to(taps_ref[CONV : CONV + 1], conv_in.shape)
    for tap in range(CONV):
        back = CONV - 1 - tap
        term = taps_ref[tap : tap + 1] * extended[halo - back : halo - back + TILE]
        if back:
            term = jnp.where((place >= start) & (place < start + back), 0.0, term)
        pre = pre + term
    pre_ref[...] = pre
    activated = pre * logistic(pre)
    both = activated[:, width:].astype(BF16)
    kq_ref[...] = both
    for part in range(TILE // CHUNK):
        rows = slice(part * CHUNK, (part + 1) * CHUNK)
        begin = step * TILE + part * CHUNK
        keys, queries = both[rows, :STATE], both[rows, STATE:]
        terms = chunk_terms(narrow[rows, 2 * STATE :], heads_ref[...], begin, start)
        _, steps, _, cumulative, entering, leaving, whole, segment = terms
        reach_ref[rows] = jnp.where(segment, 0.0, jnp.exp(offset[0:1] + cumulative))
        first = jnp.where(begin - 1 >= start, 0.0, 1.0)
        factor = jnp.broadcast_to(jnp.exp(offset[0:1]) * first, (8, LANES))
        factor_ref[part] = spread_all(factor, width)
        offset[...] = offset[...] + cumulative[CHUNK - 1 : CHUNK]
        held = state[...]
        states_ref[part] = held
        across = cumulative.T
        row, column = iota((CHUNK, CHUNK), 0), iota((CHUNK, CHUNK), 1)
        segment_row, segment_column = begin + row >= start, begin + column >= start
        hide = jnp.where((row >= column) & (segment_row == segment_column), 0.0, -1e30)
        scores = mm(queries, keys, NT)
        carried = mm_exact(queries, split_three(held))
        weighted = []
        for pair in range(width // LANES):
            lanes = slice(pair * LANES, (pair + 1) * LANES)
            sources = spread_pair(steps, pair) * activated[rows, lanes]
            high, low = split(sources)
            right = jnp.concatenate(
                [
                    jnp.concatenate([high, low], axis=1),
                    jnp.concatenate([high, jnp.zeros_like(low)], axis=1),
                ],
                axis=0,
            )
            left = []
            for head in (2 * pair, 2 * pair + 1):
                decay = jnp.exp(cumulative[:, head : head + 1] - across[head : head + 1] + hide)
                left.append(jnp.concatenate(split(scores * decay), axis=1))
            mixed = mm(jnp.concatenate(left, axis=0), right)
            mixed = mixed[:, :LANES] + mixed[:, LANES:]
            inner = jnp.where(low_lane, mixed[:CHUNK], mixed[CHUNK:])
            local_ref[rows, lanes] = (
                inner + spread_pair(entering, pair) * carried[:, lanes]
            )
            weighted.append(spread_pair(leaving, pair) * sources)
        added = mm_exact(keys, split_three(jnp.concatenate(weighted, axis=1)), TN)
        state[...] = spread_all(whole, width) * held + added

    @pl.when(step == pl.num_programs(0) - 1)
    def _():
        final_ref[0:STATE] = state[...]
        kept = jnp.where(pl.num_programs(0) * TILE - 1 >= start, 0.0, 1.0)
        factor = jnp.broadcast_to(jnp.exp(offset[0:1]) * kept, (8, LANES))
        final_ref[STATE : STATE + 8] = spread_all(factor, width)


def gate_kernel(
    incoming_ref, local_ref, kq_ref, reach_ref, gates_ref, pre_ref, skip_ref, cotangent_ref,
    output_ref, gain_ref, scanned_ref, back_ref, sums_ref,
):
    width = gates_ref.shape[1]
    low_lane = iota((TILE, LANES), 1) < 64
    carried = mm_exact(kq_ref[...], split_three(incoming_ref[...]))
    scanned = local_ref[...] + spread_all(reach_ref[...], width) * carried
    scanned_ref[...] = scanned
    pre = pre_ref[...]
    mixed = scanned + skip_ref[...] * (pre * logistic(pre))
    gates = gates_ref[...]
    gated = mixed * (gates * logistic(gates))
    back = mm(cotangent_ref[...].astype(BF16), output_ref[...])
    back_ref[...] = back
    squares = jnp.sum(gated * gated, axis=1, keepdims=True)
    products = jnp.sum(back * gain_ref[...] * gated, axis=1, keepdims=True)
    lane = iota((TILE, LANES), 1)
    both = jnp.where(lane == 0, squares, jnp.where(lane == 1, products, 0.0))
    sums_ref[...] = both.T[:2]


def gate_back_kernel(
    sums_ref, scanned_ref, kq_ref, reach_ref, gates_ref, pre_ref, skip_ref, back_ref, gain_ref,
    out_ref, mixed_grad_ref, gates_grad_ref, adjoint_ref, gain_grad_ref,
):
    step = pl.program_id(0)
    width = gates_ref.shape[1]
    low_lane = iota((TILE, LANES), 1) < 64

    @pl.when(step == 0)
    def _():
        adjoint_ref[...] = jnp.zeros_like(adjoint_ref)
        gain_grad_ref[...] = jnp.zeros_like(gain_grad_ref)

    sums = jnp.concatenate([sums_ref[...], jnp.zeros((LANES - 2, TILE), F32)], axis=0).T
    scale = lax.rsqrt(sums[:, 0:1] / INNER + norm_epsilon)
    shrink = scale * scale * scale * sums[:, 1:2] / INNER
    pre = pre_ref[...]
    mixed = scanned_ref[...] + skip_ref[...] * (pre * logistic(pre))
    gates = gates_ref[...]
    sigmoid = logistic(gates)
    silu = gates * sigmoid
    gated = mixed * silu
    unit = gated * scale
    back = back_ref[...]
    out_ref[...] = (unit * gain_ref[...]).astype(BF16)
    gain_grad_ref[0:1] = gain_grad_ref[0:1] + jnp.sum(back * unit, axis=0, keepdims=True)
    gated_grad = back * gain_ref[...] * scale - gated * shrink
    mixed_grad = gated_grad * silu
    mixed_grad_ref[...] = mixed_grad
    gates_grad = gated_grad * mixed * sigmoid * (1.0 + gates * (1.0 - sigmoid))
    gates_grad_ref[...] = gates_grad.astype(BF16)
    parts = split_three(spread_all(reach_ref[...], width) * mixed_grad)
    adjoint_ref[...] = adjoint_ref[...] + mm_exact(kq_ref[...], parts, TN)


def head_select(width):
    lane = iota((width, LANES), 0)
    head = iota((width, LANES), 1)
    return jnp.where((lane >= head * 64) & (lane < head * 64 + 64), 1.0, 0.0).astype(BF16)


def back_kernel(
    start_ref, pre_ref, kq_ref, raw_ref, mixed_grad_ref, scanned_ref, states_ref, factor_ref,
    incoming_ref, outgoing_ref, gates_grad_ref, skip_ref, heads_ref, taps_ref, conv_ref,
    grad_ref, steps_ref, narrow_ref, first_ref, last_ref, taps_grad_ref, heads_grad_ref, skip_grad_ref,
    extended, adjoint,
):
    step = pl.program_id(0)
    count = pl.num_programs(0)
    tile = count - 1 - step
    width = gates_grad_ref.shape[1]
    channels = pre_ref.shape[1]
    halo = first_ref.shape[0]
    start = start_ref[0]
    low_lane = iota((CHUNK, LANES), 1) < 64
    select = head_select(width)

    @pl.when(step == 0)
    def _():
        adjoint[...] = outgoing_ref[...]
        extended[TILE : TILE + halo] = jnp.zeros((halo, channels), F32)
        taps_grad_ref[...] = jnp.zeros_like(taps_grad_ref)
        heads_grad_ref[...] = jnp.zeros_like(heads_grad_ref)
        skip_grad_ref[...] = jnp.zeros_like(skip_grad_ref)

    @pl.when(step > 0)
    def _():
        extended[TILE : TILE + halo] = extended[0:halo]

    for part in reversed(range(TILE // CHUNK)):
        rows = slice(part * CHUNK, (part + 1) * CHUNK)
        begin = tile * TILE + part * CHUNK
        keys, queries = kq_ref[rows, :STATE], kq_ref[rows, STATE:]
        terms = chunk_terms(raw_ref[rows], heads_ref[...], begin, start)
        shifted, steps, logdecay, cumulative, entering, leaving, whole, _ = terms
        held = states_ref[part] + factor_ref[part, 0:1] * incoming_ref[...]
        later = adjoint[...]
        across = cumulative.T
        row, column = iota((CHUNK, CHUNK), 0), iota((CHUNK, CHUNK), 1)
        segment_row, segment_column = begin + row >= start, begin + column >= start
        hide = jnp.where((column >= row) & (segment_row == segment_column), 0.0, -1e30)
        scores = mm(keys, queries, NT)
        later_parts = split_three(later)
        held_parts = split_three(held)
        from_later = mm_exact(keys, later_parts)
        pre = pre_ref[rows]
        sigmoid = logistic(pre)
        values = pre[:, :width] * sigmoid[:, :width]
        mixed_grad = mixed_grad_ref[rows]
        scores_grad = jnp.zeros((CHUNK, CHUNK), F32)
        within, beyond, received, sent, expanded = [], [], [], [], []
        for pair in range(width // LANES):
            lanes = slice(pair * LANES, (pair + 1) * LANES)
            wide_steps = spread_pair(steps, pair)
            sources = wide_steps * values[:, lanes]
            high, low = split(sources)
            grad = mixed_grad[:, lanes]
            grad_high, grad_low = split(grad)
            right = jnp.concatenate(
                [
                    jnp.concatenate([grad_high, grad_low], axis=1),
                    jnp.concatenate([grad_high, jnp.zeros_like(grad_low)], axis=1),
                ],
                axis=0,
            )
            zero = jnp.zeros_like(high)
            highs = jnp.concatenate(
                [jnp.where(low_lane, high, zero), jnp.where(low_lane, zero, high)], axis=0
            )
            lows = jnp.concatenate(
                [jnp.where(low_lane, low, zero), jnp.where(low_lane, zero, low)], axis=0
            )
            products = (
                mm(highs, grad_high, NT) + mm(lows, grad_high, NT) + mm(highs, grad_low, NT)
            )
            left = []
            for index, head in enumerate((2 * pair, 2 * pair + 1)):
                decay = jnp.exp(across[head : head + 1] - cumulative[:, head : head + 1] + hide)
                left.append(jnp.concatenate(split(scores * decay), axis=1))
                part_rows = slice(index * CHUNK, (index + 1) * CHUNK)
                scores_grad = scores_grad + products[part_rows] * decay
            both = mm(jnp.concatenate(left, axis=0), right)
            both = both[:, :LANES] + both[:, LANES:]
            within.append(jnp.where(low_lane, both[:CHUNK], both[CHUNK:]))
            wide_leaving = spread_pair(leaving, pair)
            beyond.append(wide_leaving * from_later[:, lanes])
            sent.append(wide_leaving * sources)
            received.append(spread_pair(entering, pair) * grad)
            expanded.append(wide_steps)
        within = jnp.concatenate(within, axis=1)
        beyond = jnp.concatenate(beyond, axis=1)
        wide_steps = jnp.concatenate(expanded, axis=1)
        sent_parts = split_three(jnp.concatenate(sent, axis=1))
        received_parts = split_three(jnp.concatenate(received, axis=1))
        keys_grad = (
            sum(mm(piece, queries) for piece in reversed(split_three(scores_grad)))
            + mm_full(sent_parts, later_parts, NT)
        )
        queries_grad = (
            sum(mm(piece, keys) for piece in reversed(split_three(scores_grad.T)))
            + mm_full(received_parts, held_parts, NT)
        )
        wide_whole = spread_all(whole, width)
        adjoint[...] = wide_whole * later + mm_exact(queries, received_parts, TN)
        crossing = jnp.sum(wide_whole * held * later, axis=0, keepdims=True)
        stack = jnp.concatenate(
            [
                mixed_grad * scanned_ref[rows],
                values * within,
                values * beyond,
                jnp.broadcast_to(crossing, (8, width)),
            ],
            axis=0,
        )
        totals = sum(mm(piece, select) for piece in reversed(split_three(stack)))
        own = totals[:CHUNK]
        near = totals[CHUNK : 2 * CHUNK]
        far = totals[2 * CHUNK : 3 * CHUNK]
        crossing = totals[3 * CHUNK : 3 * CHUNK + 1]
        logdecay_grad = (
            triangle_sum(column >= row, own - steps * near)
            + triangle_sum(column < row, steps * far)
            + crossing
        )
        rate = jnp.exp(heads_ref[1:2])
        steps_grad = near + far - rate * logdecay_grad
        raw_grad = steps_grad * logistic(shifted)
        heads_grad_ref[0:1] = heads_grad_ref[0:1] + jnp.sum(raw_grad, axis=0, keepdims=True)
        heads_grad_ref[1:2] = heads_grad_ref[1:2] + jnp.sum(
            logdecay_grad * logdecay, axis=0, keepdims=True
        )
        skip_grad_ref[0:1] = skip_grad_ref[0:1] + jnp.sum(
            values * mixed_grad, axis=0, keepdims=True
        )
        values_grad = wide_steps * (within + beyond) + skip_ref[...] * mixed_grad
        activated_grad = jnp.concatenate([values_grad, keys_grad, queries_grad], axis=1)
        extended[rows] = activated_grad * sigmoid * (1.0 + pre * (1.0 - sigmoid))
        steps_ref[rows] = raw_grad.astype(BF16)

    grad_ref[:, :width] = gates_grad_ref[...]
    place = tile * TILE + iota((TILE, 1), 0)
    edge = jnp.where(start >= count * TILE, 1 << 30, start)
    conv_in = conv_ref[...].astype(F32)
    total = jnp.zeros((TILE, channels), F32)
    for tap in range(CONV):
        ahead = CONV - 1 - tap
        moved = extended[ahead : ahead + TILE]
        if ahead:
            moved = jnp.where((place < edge) & (place + ahead >= edge), 0.0, moved)
        total = total + taps_ref[tap : tap + 1] * moved
        taps_grad_ref[tap : tap + 1] = taps_grad_ref[tap : tap + 1] + jnp.sum(
            conv_in * moved, axis=0, keepdims=True
        )
    taps_grad_ref[CONV : CONV + 1] = taps_grad_ref[CONV : CONV + 1] + jnp.sum(
        extended[0:TILE], axis=0, keepdims=True
    )
    grad_ref[:, width:] = total[:, :width].astype(BF16)
    narrow_ref[...] = total[:, width:]

    @pl.when(step == 0)
    def _():
        last_ref[...] = total[TILE - halo :]

    @pl.when(step == count - 1)
    def _():
        first_ref[...] = extended[0:halo]


def rows_spec(rows, width):
    return pl.BlockSpec((rows, width), lambda step: (step, 0))


def whole_spec(shape):
    return pl.BlockSpec(shape, lambda step: (0,) * len(shape))


def like(shape, dtype=F32):
    return jax.ShapeDtypeStruct(shape, dtype)


def cost(microseconds):
    return pl.CostEstimate(
        flops=microseconds * 10**9, bytes_accessed=microseconds * 3 * 10**6, transcendentals=0
    )


def settings():
    return pltpu.CompilerParams(vmem_limit_bytes=48 * 1024 * 1024)


SCALAR = pl.BlockSpec(memory_space=pltpu.SMEM)


def forward_call(start, rounded, tail, wide, small, taps, heads):
    rows, depth = rounded.shape
    width = wide.shape[1] // 3
    channels = width + 2 * STATE
    parts = TILE // CHUNK
    return pl.pallas_call(
        forward_kernel,
        grid=(rows // TILE,),
        in_specs=[SCALAR, rows_spec(TILE, depth)]
        + [whole_spec(tail.shape), whole_spec((depth, 2 * width))]
        + [whole_spec(a.shape) for a in (small, taps, heads)],
        out_specs=[
            rows_spec(TILE, width),
            rows_spec(TILE, channels),
            rows_spec(TILE, channels),
            rows_spec(TILE, 2 * STATE),
            rows_spec(TILE, LANES),
            rows_spec(TILE, width),
            pl.BlockSpec((parts, STATE, width), lambda step: (step, 0, 0)),
            rows_spec(TILE, LANES),
            pl.BlockSpec((parts, 8, width), lambda step: (step, 0, 0)),
            whole_spec((STATE + 8, width)),
        ],
        out_shape=[
            like((rows, width)),
            like((rows, channels)),
            like((rows, channels), BF16),
            like((rows, 2 * STATE), BF16),
            like((rows, LANES)),
            like((rows, width)),
            like((rows // CHUNK, STATE, width)),
            like((rows, LANES)),
            like((rows // CHUNK, 8, width)),
            like((STATE + 8, width)),
        ],
        scratch_shapes=[
            pltpu.VMEM((TILE + tail.shape[0], channels), F32),
            pltpu.VMEM((STATE, width), F32),
            pltpu.VMEM((8, LANES), F32),
        ],
        compiler_params=settings(),
        cost_estimate=cost(33),
        name="scan_forward",
    )(start, rounded, tail, wide, small, taps, heads)


def gate_call(incoming, local, kq, reach, gates, pre, skip, cotangent, wide, gain):
    rows, width = gates.shape
    tile = rows_spec(TILE, width)
    return pl.pallas_call(
        gate_kernel,
        grid=(rows // TILE,),
        in_specs=[
            whole_spec(incoming.shape),
            tile,
            pl.BlockSpec((TILE, STATE), lambda step: (step, 1)),
            rows_spec(TILE, LANES),
            tile,
            tile,
            whole_spec(skip.shape),
            rows_spec(TILE, cotangent.shape[1]),
            pl.BlockSpec((wide.shape[0], width), lambda step: (0, 2)),
            whole_spec(gain.shape),
        ],
        out_specs=[tile, tile, pl.BlockSpec((2, TILE), lambda step: (0, step))],
        out_shape=[like((rows, width)), like((rows, width)), like((2, rows))],
        compiler_params=settings(),
        cost_estimate=cost(15),
        name="gate_forward",
    )(incoming, local, kq, reach, gates, pre, skip, cotangent, wide, gain)


def gate_back_call(sums, scanned, kq, reach, gates, pre, skip, back, gain):
    rows, width = gates.shape
    tile = rows_spec(TILE, width)
    return pl.pallas_call(
        gate_back_kernel,
        grid=(rows // TILE,),
        in_specs=[
            pl.BlockSpec((2, TILE), lambda step: (0, step)),
            tile,
            pl.BlockSpec((TILE, STATE), lambda step: (step, 1)),
            rows_spec(TILE, LANES),
            tile,
            tile,
            whole_spec(skip.shape),
            tile,
            whole_spec(gain.shape),
        ],
        out_specs=[tile, tile, tile, whole_spec((STATE, width)), whole_spec((8, width))],
        out_shape=[
            like((rows, width), BF16),
            like((rows, width)),
            like((rows, width), BF16),
            like((STATE, width)),
            like((8, width)),
        ],
        compiler_params=settings(),
        cost_estimate=cost(12),
        name="gate_backward",
    )(sums, scanned, kq, reach, gates, pre, skip, back, gain)


def back_call(
    start, pre, kq, raw, mixed_grad, scanned, states, factor, incoming, outgoing, gates_grad, skip,
    heads, taps, conv_in,
):
    rows, width = gates_grad.shape
    channels = pre.shape[1]
    count = rows // TILE
    parts = TILE // CHUNK

    def tile(columns):
        return pl.BlockSpec((TILE, columns), lambda step: (count - 1 - step, 0))

    def blocks(height):
        return pl.BlockSpec((parts, height, width), lambda step: (count - 1 - step, 0, 0))

    return pl.pallas_call(
        back_kernel,
        grid=(count,),
        in_specs=[
            SCALAR,
            tile(channels),
            tile(2 * STATE),
            tile(LANES),
            tile(width),
            tile(width),
            blocks(STATE),
            blocks(8),
            whole_spec(incoming.shape),
            whole_spec(outgoing.shape),
            tile(width),
            whole_spec(skip.shape),
            whole_spec(heads.shape),
            whole_spec(taps.shape),
            tile(channels),
        ],
        out_specs=[
            tile(2 * width),
            tile(LANES),
            tile(2 * STATE),
            whole_spec((16, channels)),
            whole_spec((16, channels)),
            whole_spec((8, channels)),
            whole_spec((8, LANES)),
            whole_spec((8, width)),
        ],
        out_shape=[
            like((rows, 2 * width), BF16),
            like((rows, LANES), BF16),
            like((rows, 2 * STATE)),
            like((16, channels)),
            like((16, channels)),
            like((8, channels)),
            like((8, LANES)),
            like((8, width)),
        ],
        scratch_shapes=[
            pltpu.VMEM((TILE + 16, channels), F32),
            pltpu.VMEM((STATE, width), F32),
        ],
        compiler_params=settings(),
        cost_estimate=cost(48),
        name="scan_backward",
    )(
        start, pre, kq, raw, mixed_grad, scanned, states, factor, incoming, outgoing, gates_grad,
        skip, heads, taps, conv_in,
    )


def adamw(weight, gradient, first, second, rate, shrink):
    first_new = moment_decay * first + (1.0 - moment_decay) * gradient
    second_new = moment_decay * second + (1.0 - moment_decay) * gradient * gradient
    correction = 1.0 - moment_decay**STEP
    ratio = first_new / correction / (jnp.sqrt(second_new / correction) + adam_epsilon)
    return (weight - rate * (ratio + shrink * weight), first_new, second_new)


def on_device(
    tokens,
    cotangent,
    sequence_starts,
    norm_gain,
    inner_weight,
    state_weight,
    step_weight,
    inner_params,
    state_conv,
    head_params,
    output_weight,
    first_norm_gain,
    second_norm_gain,
    first_inner_weight,
    second_inner_weight,
    first_state_weight,
    second_state_weight,
    first_step_weight,
    second_step_weight,
    first_inner_params,
    second_inner_params,
    first_state_conv,
    second_state_conv,
    first_head_params,
    second_head_params,
    first_output_weight,
    second_output_weight,
):
    rows, width = tokens.shape
    inner_local = inner_weight.shape[2]
    state_local = state_weight.shape[2]
    heads_local = step_weight.shape[1]
    head_place = lax.axis_index("head")
    start = sequence_starts[0]
    channels = inner_local + 2 * STATE
    split_two = 2 * inner_local
    wide = jnp.concatenate([inner_weight.reshape(-1, split_two), output_weight.T], axis=1)
    wide = lax.all_gather(wide.astype(jnp.bfloat16), "seq", axis=0, tiled=True)
    inner_full, output_full = wide[:, :split_two], wide[:, split_two:]
    own_rows = state_weight.shape[0]
    side = jnp.concatenate(
        [
            state_weight.reshape(own_rows, 2, state_local),
            state_conv,
            jnp.zeros((3, 2, state_local), jnp.float32),
        ],
        axis=0,
    )
    side = lax.all_gather(side.reshape(own_rows + 8, 2 * state_local), "head")
    side = side.reshape(-1, own_rows + 8, 2, state_local).transpose(1, 2, 0, 3)
    side = side.reshape(own_rows + 8, 2 * STATE)
    narrow = jnp.concatenate(
        [side[:own_rows], step_weight, jnp.zeros((own_rows, LANES - heads_local), jnp.float32)],
        axis=1,
    )
    small_full = lax.all_gather(narrow.astype(jnp.bfloat16), "seq", axis=0, tiled=True)
    taps = jnp.concatenate([inner_params[: CONV + 1], side[own_rows : own_rows + CONV + 1]], axis=1)
    taps = jnp.pad(taps, ((0, 8 - CONV - 1), (0, 0)))
    heads = jnp.pad(head_params[:2], ((0, 6), (0, LANES - heads_local)))
    skip = jnp.repeat(head_params[2], inner_local // heads_local)[None]
    gate_gain = inner_params[CONV + 1 : CONV + 2]
    places = jnp.arange(rows - 16, rows, dtype=jnp.int32)
    tail_keep = ((places >= start) == (start <= rows - 1))[:, None]
    recent = (jnp.arange(16) >= 16 - CONV + 1)[:, None]
    tail = passed_along(jnp.where(tail_keep & recent, tokens[rows - 16 :], 0.0), "seq", 1)
    inverse = lax.rsqrt(jnp.mean(tokens * tokens, axis=1, keepdims=True) + norm_epsilon)
    rounded = (tokens * inverse * norm_gain).astype(jnp.bfloat16)
    tail_scale = lax.rsqrt(jnp.mean(tail * tail, axis=1, keepdims=True) + norm_epsilon)
    tail = (tail * tail_scale * norm_gain).astype(jnp.bfloat16)
    begin = start[None]
    (
        gates, pre, conv_in, kq, raw, local, states, reach, factor, final
    ) = forward_call(
        begin, rounded, tail, wide, small_full, taps, heads
    )
    incoming = carried_in(final, "seq", False)
    scanned, back, sums = gate_call(
        incoming, local, kq, reach, gates, pre, skip, cotangent, wide, gate_gain
    )
    sums = lax.psum(sums, "head")
    gate_out, mixed_grad, gates_grad, adjoint, gain_grad = gate_back_call(
        sums, scanned, kq, reach, gates, pre, skip, back, gate_gain
    )
    outgoing = carried_in(jnp.concatenate([adjoint, final[STATE:]], axis=0), "seq", True)
    partial_out = lax.dot_general(
        gate_out, output_full, (((1,), (1,)), ((), ())), preferred_element_type=jnp.float32
    )
    branch = LineSum(partial_out, "head")
    branch.send(0)
    output_weight_grad = lax.dot_general(
        cotangent.astype(jnp.bfloat16),
        gate_out,
        (((0,), (0,)), ((), ())),
        preferred_element_type=jnp.float32,
    )
    output_total = lax.psum_scatter(output_weight_grad, "seq", scatter_dimension=0, tiled=True)
    outgoing = outgoing + nothing(output_weight_grad, *branch.sent)
    (
        wide_grad, step_grad, narrow_grad, first_grad, last_grad, taps_grad, heads_grad, skip_grad
    ) = back_call(
        begin, pre, kq, raw, mixed_grad, scanned, states, factor, incoming, outgoing, gates_grad,
        skip, heads, taps, conv_in,
    )
    output_total = (output_total + nothing(first_grad)).T
    branch.receive(first_grad)
    branch.send(1)
    early = (jnp.arange(8) < jnp.minimum(start, CONV - 1))[:, None]
    halo = passed_along(jnp.where(early, first_grad[:8], 0.0), "seq", -1)
    ahead_rows = jnp.concatenate([jnp.zeros((16, channels), jnp.float32), halo], axis=0)
    last_conv = conv_in[rows - 16 :].astype(jnp.float32)
    extra = []
    for tap in range(CONV - 1):
        ahead = CONV - 1 - tap
        moved = jnp.where(tail_keep, ahead_rows[ahead : ahead + 16], 0.0)
        last_grad = last_grad + taps[tap] * moved
        extra.append(jnp.sum(last_conv * moved, axis=0))
    taps_grad = taps_grad[: CONV + 1] + jnp.pad(jnp.stack(extra), ((0, 2), (0, 0)))
    wide_grad = lax.dynamic_update_slice(
        wide_grad, last_grad[:, :inner_local].astype(jnp.bfloat16), (rows - 16, inner_local)
    )
    narrow_grad = lax.dynamic_update_slice(narrow_grad, last_grad[:, inner_local:], (rows - 16, 0))
    head_count = lax.axis_size("head")
    piece = rows // (2 * head_count)
    narrow_grad = narrow_grad.reshape(2, head_count, piece, 2 * STATE)
    narrow_grad = jnp.stack(
        [
            narrow_grad[0, jnp.array([reversed_bits(z, head_count) for z in range(head_count)])],
            narrow_grad[1],
        ],
        axis=1,
    )
    state_grad = lax.psum_scatter(
        narrow_grad.reshape(rows, 2 * STATE), "head", scatter_dimension=0, tiled=True
    ).astype(jnp.bfloat16)
    own_rows = [
        reversed_bits(head_place, head_count) * piece,
        rows // 2 + head_place * piece,
    ]
    own_rounded = jnp.concatenate(
        [lax.dynamic_slice_in_dim(rounded, first, piece, 0) for first in own_rows]
    )
    normed_part = lax.dot_general(
        wide_grad,
        inner_full,
        (((1,), (1,)), ((), ())),
        preferred_element_type=jnp.float32,
    ) + lax.dot_general(
        step_grad,
        small_full[:, 2 * STATE :],
        (((1,), (1,)), ((), ())),
        preferred_element_type=jnp.float32,
    )
    normed_state = lax.dot_general(
        state_grad,
        small_full[:, : 2 * STATE],
        (((1,), (1,)), ((), ())),
        preferred_element_type=jnp.float32,
    )
    state_matrix = lax.dot_general(
        own_rounded, state_grad, (((0,), (0,)), ((), ())), preferred_element_type=jnp.float32
    )
    matrix_grad = lax.dot_general(
        rounded,
        jnp.concatenate(
            [
                wide_grad,
                step_grad[:, :heads_local],
            ],
            axis=1,
        ),
        (((0,), (0,)), ((), ())),
        preferred_element_type=jnp.float32,
    )
    matrix_grad = jnp.concatenate([state_matrix, matrix_grad], axis=1)
    own_tokens = jnp.concatenate(
        [lax.dynamic_slice_in_dim(tokens * inverse, first, piece, 0) for first in own_rows]
    )
    norm_gain_grad = jnp.sum(normed_part * tokens * inverse, axis=0) + jnp.sum(
        normed_state * own_tokens, axis=0
    )
    normed = LineSum(normed_part, "head")
    normed.send(0)
    for level in range(1, branch.levels):
        branch.receive(*normed.sent)
        if level < branch.levels - 1:
            branch.send(level + 1)
    branch.pack()
    branch.share(branch.levels - 1)
    matrix_total = lax.psum_scatter(matrix_grad, "seq", scatter_dimension=0, tiled=True)
    normed.receive(*branch.sent)
    for level in range(1, normed.levels):
        normed.send(level)
        if level < normed.levels - 1:
            normed.receive()
    shared = jnp.concatenate(
        [norm_gain_grad.reshape(-1, LANES), taps_grad[:, inner_local:].reshape(-1, LANES)], axis=0
    )
    shared = shared + nothing(*normed.sent)
    gain_rows = width // LANES
    own_gain = jnp.concatenate([taps_grad[:, :inner_local], gain_grad[:1]], axis=0)
    skip_sums = jnp.sum(skip_grad[0].reshape(heads_local, -1), axis=1)
    head_rows = jnp.concatenate([heads_grad[:2], jnp.pad(skip_sums, (0, LANES - heads_local))[None]])
    totals = lax.psum(
        jnp.concatenate([shared, own_gain.reshape(-1, LANES), head_rows], axis=0), "seq"
    )
    shared_rows = gain_rows + 2 * (CONV + 1)
    for level in reversed(range(1, branch.levels)):
        branch.join(level, matrix_grad, *normed.sent)
        branch.share(level - 1)
    normed.receive(totals, *branch.sent)
    normed.parts = [part + more for part, more in zip(normed.parts, jnp.split(normed_state, 2))]
    normed.pack()
    own_rows = matrix_total.shape[0]
    over_heads = lax.psum(
        jnp.concatenate(
            [
                matrix_total[:, : 2 * STATE],
                jnp.pad(totals[:shared_rows].reshape(-1, 2 * STATE), ((0, 7), (0, 0))),
            ],
            axis=0,
        ),
        "head",
    )
    state_total = over_heads[:own_rows].reshape(-1, 2, STATE)
    shared = over_heads[own_rows : own_rows + shared_rows // 2].reshape(shared_rows, LANES)
    normed.share(normed.levels - 1)
    for level in reversed(range(1, normed.levels)):
        normed.join(level, matrix_total)
        normed.share(level - 1)
    branch.join(0, *normed.sent)
    output = tokens + branch.result()
    normed.join(0)
    normed_grad = normed.result()
    scaled_grad = normed_grad * norm_gain
    input_gradient = (
        cotangent
        + inverse * scaled_grad
        - tokens * inverse**3 * jnp.mean(scaled_grad * tokens, axis=1, keepdims=True)
    )
    state_total = lax.dynamic_slice_in_dim(state_total, head_place * state_local, state_local, 2)
    matrix_total = matrix_total[:, 2 * STATE :]
    inner_total = matrix_total[:, :split_two].reshape(-1, 2, inner_local)
    step_total = matrix_total[:, split_two:]
    gain_total = shared[:gain_rows].reshape(-1)
    conv_total = lax.dynamic_slice_in_dim(
        shared[gain_rows:].reshape(CONV + 1, 2, STATE),
        head_place * state_local,
        state_local,
        2,
    )
    params_total = totals[shared_rows:-3].reshape(CONV + 2, inner_local)
    head_sum = totals[-3:, :heads_local]
    matrix_rate = 2.0 * D ** (-0.5)
    output_rate = 2.0 * INNER ** (-0.5)
    gain_next = adamw(norm_gain, gain_total, first_norm_gain, second_norm_gain, 0.5, 0.0)
    inner_next = adamw(
        inner_weight,
        inner_total,
        first_inner_weight,
        second_inner_weight,
        matrix_rate,
        weight_decay,
    )
    state_next = adamw(
        state_weight,
        state_total,
        first_state_weight,
        second_state_weight,
        matrix_rate,
        weight_decay,
    )
    step_next = adamw(
        step_weight, step_total, first_step_weight, second_step_weight, matrix_rate, weight_decay
    )
    params_next = adamw(
        inner_params, params_total, first_inner_params, second_inner_params, 0.5, 0.0
    )
    conv_next = adamw(state_conv, conv_total, first_state_conv, second_state_conv, 0.5, 0.0)
    head_next = adamw(head_params, head_sum, first_head_params, second_head_params, 3.0, 0.0)
    output_next = adamw(
        output_weight,
        output_total,
        first_output_weight,
        second_output_weight,
        output_rate,
        weight_decay,
    )
    return (
        output,
        input_gradient,
        gain_next[0],
        gain_next[1],
        gain_next[2],
        inner_next[0],
        inner_next[1],
        inner_next[2],
        state_next[0],
        state_next[1],
        state_next[2],
        step_next[0],
        step_next[1],
        step_next[2],
        params_next[0],
        params_next[1],
        params_next[2],
        conv_next[0],
        conv_next[1],
        conv_next[2],
        head_next[0],
        head_next[1],
        head_next[2],
        output_next[0],
        output_next[1],
        output_next[2],
    )


def solution(mesh):
    placed = (
        P("seq", None),
        P("seq", None),
        P("seq"),
        P(),
        P("seq", None, "head"),
        P("seq", None, "head"),
        P("seq", "head"),
        P(None, "head"),
        P(None, None, "head"),
        P(None, "head"),
        P("head", "seq"),
        P(),
        P(),
        P("seq", None, "head"),
        P("seq", None, "head"),
        P("seq", None, "head"),
        P("seq", None, "head"),
        P("seq", "head"),
        P("seq", "head"),
        P(None, "head"),
        P(None, "head"),
        P(None, None, "head"),
        P(None, None, "head"),
        P(None, "head"),
        P(None, "head"),
        P("head", "seq"),
        P("head", "seq"),
    )
    return jax.shard_map(
        on_device,
        mesh=mesh,
        in_specs=placed,
        out_specs=(
            P("seq", None),
            P("seq", None),
            P(),
            P(),
            P(),
            P("seq", None, "head"),
            P("seq", None, "head"),
            P("seq", None, "head"),
            P("seq", None, "head"),
            P("seq", None, "head"),
            P("seq", None, "head"),
            P("seq", "head"),
            P("seq", "head"),
            P("seq", "head"),
            P(None, "head"),
            P(None, "head"),
            P(None, "head"),
            P(None, None, "head"),
            P(None, None, "head"),
            P(None, None, "head"),
            P(None, "head"),
            P(None, "head"),
            P(None, "head"),
            P("head", "seq"),
            P("head", "seq"),
            P("head", "seq"),
        ),
        check_vma=False,
    )
```

time: 1330 us -> 673 us (0.51)
  waiting for transfers between devices: 774 us -> 196 us
  matrix products: 165 us -> 35.6 us
  Pallas kernels: 0 us -> 107 us
  other arithmetic: 191 us -> 119 us
  starting transfers between devices: 4.72 us -> 35.2 us
  local copies, waits for them, and re-layouts: 90.4 us -> 68 us
  between operations: 17.5 us -> 30.8 us
    psum x1, waiting for transfers between devices: 563 us -> 49.6 us  [on_device(): lax.psum(jnp.concatenate([matrix_total[:, :2 * STATE], jnp.pad(totals[:sh...]
    dot_general x18 -> x7, matrix products: 165 us -> 35.6 us  [the longest x1 9.71 us: on_device(): lax.dot_general(rounded, jnp.concatenate([wide_grad, step_grad[:, :heads_...]
    pallas_call x0 -> x4, Pallas kernels: none -> 107 us  [the longest x1 47.6 us: back_call(): pl.pallas_call(back_kernel, grid=(count,), in_specs=[SCALAR, tile(channel...]
    ppermute x0 -> x16, waiting for transfers between devices: none -> 94.4 us  [the longest x8 59.3 us: share(): self.flight.append(lax.ppermute(part, self.axis, pairs))]
    unnamed x12 -> x7, waiting for transfers between devices: 82.9 us -> 0.11 us
    reduce_scatter x4 -> x3, waiting for transfers between devices: 79.9 us -> 24.1 us  [the longest x1 24.1 us: on_device(): lax.psum_scatter(narrow_grad.reshape(rows, 2 * STATE), 'head', scatter_di...]
    reduce_sum x14 -> x4, other arithmetic: 54.5 us -> 2.6 us  [the longest x1 1 us: on_device(): jnp.mean(scaled_grad * tokens, axis=1, keepdims=True)]
    another operation x12 -> x3, other arithmetic: 51.5 us -> 4.27 us  [the longest x1 2.97 us: on_device(): jnp.stack([narrow_grad[0, jnp.array([reversed_bits(z, head_count) for z i...]
  transfers between devices with their start and end apart: 13 -> 25, of which waited for: 7 -> 6; matrix products, arithmetic and copies ran while one was open for 17% -> 25% of each run, Pallas kernels for 0% -> 7%
where the time goes in v1:
time: 673 us; the launch traced here: 663 us
  waiting for transfers between devices  196 us (29%)
  other arithmetic  119 us (18%)
  Pallas kernels  107 us (16%)
  blocking collectives  70.8 us (11%)
  local copies, waits for them, and re-layouts  68 us (10%)
  matrix products  35.6 us (5%)
  starting transfers between devices  35.2 us (5%)
  between operations  30.8 us (5%)
    ppermute x8, waiting for transfers between devices, share(): self.flight.append(lax.ppermute(part, self.axis, pairs))  59.3 us
    psum x1, waiting for transfers between devices, on_device(): lax.psum(jnp.concatenate([matrix_total[:, :2 * STATE], jnp.pad(totals[:sh...  49.6 us
    pallas_call x1, Pallas kernels, back_call(): pl.pallas_call(back_kernel, grid=(count,), in_specs=[SCALAR, tile(channel...  47.6 us
    ppermute x8, waiting for transfers between devices, halves_given(): return (kept, message, lax.ppermute(message, axis, pairs))  35.1 us
    unnamed x186, local copies, waits for them, and re-layouts  34.6 us
    pallas_call x1, Pallas kernels, forward_call(): pl.pallas_call(forward_kernel, grid=(rows // TILE,), in_specs=[SCALAR, ro...  32.9 us
    all_gather x2, waiting for transfers between devices, carried_in(): parts = lax.all_gather(part, axis)  27.8 us
    reduce_scatter x1, waiting for transfers between devices, on_device(): lax.psum_scatter(narrow_grad.reshape(rows, 2 * STATE), 'head', scatter_di...  24.1 us
  transfers between devices with their start and end apart: 25, of which 6 were waited for; matrix products, arithmetic and copies ran while one was open for 25% of the time, Pallas kernels for 7%

profile of v1, /device:TPU:0, one launch (start us, length us, event | category | flops | bytes accessed | tf_op | source)
XLA Modules:
  0.0 662.9 jit_solution(138946458813262265)
XLA Ops:
  15.2 15.5 %all_gather.22 = f32[4,136,64]{1,2,0:T(8,128)S(1)} all-gather(f32[1,136,64]{1,2,0:T(8,128)S(1)} %bitcast.248), channel_id=1, replica_groups=mesh['seq'=8,'head'=4] {'head'}, dimensions={0}, use_global_device_ids=true | all-gather | bytes 174080 | tf_op jit(solution)/shard_map/all_gather | solution.py:820
  31.4 14.0 %all_gather.23.small_ref = bf16[1024,384]{1,0:T(8,128)(2,1)S(1)} all-gather(bf16[128,384]{1,0:T(8,128)(2,1)S(1)} %maximum_maximum_fusion), channel_id=1, replica_groups=mesh['seq'=8,'head'=4] {'seq'}, dimensions={0}, use_global_device_ids=true | all-gather | bytes 884736 | tf_op jit(solution)/shard_map/all_gather | solution.py:827
  45.4 4.3 multiply_reduce_fusion.2
  51.3 5.1 multiply_convert_fusion
  56.7 32.9 %scan_forward.1 = (f32[2048,512]{1,0:T(8,128)}, f32[2048,768]{1,0:T(8,128)}, bf16[2048,768]{1,0:T(8,128)(2,1)}, bf16[2048,256]{1,0:T(8,128)(2,1)S(1)}, f32[2048,...) custom-call(s32[1]{0:T(128)} %copy.204.start_ref, ...), custom_call_target="tpu_custom_call" | custom-call | flops 32999999488 | bytes 99000000 | tf_op jit(solution)/shard_map/scan_forward/pallas_call | solution.py:597
  92.4 27.8 %all-gather.8.cloned.1.call-done = f32[1088,512]{1,0:T(8,128)} async-done(((f32[136,512]{1,0:T(8,128)}), f32[1088,512]{1,0:T(8,128)}) %all-gather.8.cloned.1.call-update) | async-done | bytes 2228240 | tf_op jit(solution)/shard_map/all_gather | solution.py:32
  126.9 14.0 %gate_forward.1 = (f32[2048,512]{1,0:T(8,128)}, f32[2048,512]{1,0:T(8,128)}, f32[2,2048]{1,0:T(2,128)S(1)}) custom-call(f32[128,512]{1,0:T(8,128)S(1)} %fusion.40.incoming_ref, f32[2048,512]{1,0:T(8,128)} %get-tuple-element.56.local_ref, bf16[2048,256]{1,0:T(8,128)(2,1)S(1)} %get-tuple-element.53.kq_ref, f32[2048,128]{1,0:T(8,128)S(1)} %get-tuple-element.57.reach_ref, ...), custom_call_target="tpu_custom_call" | custom-call | flops 15000000512 | bytes 45000000 | tf_op jit(solution)/shard_map/gate_forward/pallas_call | solution.py:641
  141.0 18.7 %psum.21.sums_ref = f32[2,2048]{1,0:T(2,128)S(1)} all-reduce(f32[2,2048]{1,0:T(2,128)S(1)} %get-tuple-element.59), channel_id=1, replica_groups=mesh['seq'=8,'head'=4] {'head'}, use_global_device_ids=true, to_apply=%region_2.3 | all-reduce | flops 4096 | bytes 32768 | tf_op jit(solution)/shard_map/psum | solution.py:851
  162.1 12.6 %gate_backward.1 = (bf16[2048,512]{1,0:T(8,128)(2,1)S(1)}, f32[2048,512]{1,0:T(8,128)}, bf16[2048,512]{1,0:T(8,128)(2,1)}, f32[128,512]{1,0:T(8,128)S(1)}, f32[8,512]{1,0:T(8,128)S(1)}) custom-call(f32[2,2048]{1,0:T(2,128)S(1)} %psum.21.sums_ref, f32[2048,512]{1,0:T(8,128)} %get-tuple-element.60.scanned_ref, bf16[2048,256]{1,0:T(8,128)(2,1)S(1)} %copy-done.10, ...), custom_call_target="tpu_custom_call" | custom-call | flops 12000000000 | bytes 36000000 | tf_op jit(solution)/shard_map/gate_backward/pallas_call | solution.py:667
  183.1 3.1 constant_dynamic-slice_fusion.1
  186.8 7.1 %fusion.9 = f32[1024,512]{1,0:T(8,128)} fusion(bf16[2048,512]{1,0:T(8,128)(2,1)S(1)} %get-tuple-element.66, f32[2048,1024]{1,0:T(8,128)} %cotangent_ref.1), kind=kOutput, calls=%fused_computation.42 | convolution fusion | flops 2149580800 | bytes 12582912 | tf_op jit(solution)/shard_map/dot_general | solution.py:861
  195.7 3.8 fusion.12
  220.0 47.6 %scan_backward.1 = (bf16[2048,1024]{1,0:T(8,128)(2,1)}, bf16[2048,128]{1,0:T(8,128)(2,1)S(1)}, f32[2048,256]{1,0:T(8,128)S(1)}, f32[16,768]{1,0:T(8,128)S(1)}, f...) custom-call(s32[1]{0:T(128)} %copy.204.start_ref, ...), custom_call_target="tpu_custom_call" | custom-call | flops 48000000000 | bytes 144000000 | tf_op jit(solution)/shard_map/scan_backward/pallas_call | solution.py:710
  277.4 12.7 %collective-permute-start.1 = (f32[8,768]{1,0:T(8,128)S(1)}, f32[8,768]{1,0:T(8,128)S(1)}, u32[]{:S(2)}, u32[]{:S(2)}) collective-permute-start(f32[8,768]{1,0:T(8,128)S(1)} %slice_select_fusion.1), channel_id=1, source_target_pairs={{4,0},{8,4},{12,8},{16,12},{20,16},{24,20},{28,24},{5,1},{9,5},{13... | collective-permute-start | bytes 73736 | tf_op jit(solution)/shard_map/ppermute | solution.py:26
  311.2 3.0 pad_maximum_fusion.1
  314.3 7.0 %fusion.6 = f32[2048,1024]{1,0:T(8,128)S(1)} fusion(bf16[2048,1024]{1,0:T(8,128)(2,1)} %fusion.66, bf16[1024,1536]{1,0:T(8,128)(2,1)} %all-gather.6.cloned.1.call-done.inner_ref.output_ref), kind=kOutput, calls=%fused_computation.25 | convolution fusion | flops 4294967296 | bytes 14680064 | tf_op jit(solution)/shard_map/dot_general | solution.py:913
  321.3 4.4 multiply_reduce_fusion.1
  332.5 9.7 %fusion = f32[1024,1032]{1,0:T(8,128)} fusion(bf16[2048,1024]{1,0:T(8,128)(2,1)S(1)} %copy-done.36, bf16[2048,8]{1,0:T(8,128)(2,1)S(1)} %bitcast.222, bf16[2048,1024]{1,0:T(8,128)(2,1)} %fusion.66), kind=kOutput, calls=%fused_computation.9 | convolution fusion | flops 4336975872 | bytes 12648448 | tf_op jit(solution)/shard_map/dot_general | solution.py:933
  342.2 24.1 %reduce-scatter.4.cloned.1.call-done = f32[512,256]{1,0:T(8,128)} async-done(((f32[2048,256]{1,0:T(8,128)}), f32[512,256]{1,0:T(8,128)}) %reduce-scatter.4.cloned.1.call-update) | async-done | bytes 524304 | tf_op jit(solution)/shard_map/reduce_scatter | solution.py:903
  368.8 5.2 pad_maximum_fusion
  378.5 2.7 collective-permute-start.2
  393.0 35.1 %collective-permute-done.8 = f16[528,1024]{1,0:T(8,128)(2,1)S(1)} collective-permute-done((f16[528,1024]{1,0:T(8,128)(2,1)S(1)}, f16[528,1024]{1,0:T(8,128)(2,1)S(1)}, u32[]{:S(2)}, u32[]{:S(2)}) %collective-permute-start.8) | collective-permute-done | bytes 1081376 | tf_op jit(solution)/shard_map/ppermute | solution.py:72
  440.3 24.6 %collective-permute-done.10 = f16[1,272,1024]{2,1,0:T(8,128)(2,1)} collective-permute-done((f16[1,272,1024]{2,1,0:T(8,128)(2,1)S(1)}, f16[1,272,1024]{2,1,0:T(8,128)(2,1)}, u32[]{:S(2)}, u32[]{:S(2)}) %collective-permute-start.10) | collective-permute-done | bytes 557088 | tf_op jit(solution)/shard_map/ppermute | solution.py:130
  464.9 2.7 maximum_select_fusion.5
  477.1 22.6 %psum.22 = f32[45,128]{1,0:T(8,128)S(1)} all-reduce(f32[45,128]{1,0:T(8,128)S(1)} %pad_maximum_fusion.13), channel_id=1, replica_groups=mesh['seq'=8,'head'=4] {'seq'}, use_global_device_ids=true, to_apply=%region_21.22 | all-reduce | flops 5760 | bytes 46080 | tf_op jit(solution)/shard_map/psum | solution.py:974
  512.9 34.7 %collective-permute-done.13 = f16[1,272,1024]{2,1,0:T(8,128)(2,1)S(1)} collective-permute-done((f16[1,272,1024]{2,1,0:T(8,128)(2,1)S(1)}, f16[1,272,1024]{2,1,0:T(8,128)(2,1)S(1)}, u32[]{:S(2)}, u32[]{:S(2)}) %collective-permute-start.13) | collective-permute-done | bytes 557088 | tf_op jit(solution)/shard_map/ppermute | solution.py:130
  557.7 3.5 maximum_select_fusion.1
  561.3 3.5 maximum_select_fusion
  570.1 2.8 multiply_subtract_fusion.1
  573.7 49.6 %all-reduce.9.cloned.1.call-done = f32[144,256]{1,0:T(8,128)} async-done(((f32[144,256]{1,0:T(8,128)}), f32[144,256]{1,0:T(8,128)}) %all-reduce.9.cloned.1.call-update) | async-done | bytes 147472 | tf_op jit(solution)/shard_map/psum | solution.py:985
  627.8 2.7 maximum_select_fusion.2
  637.5 18.1 %multiply_subtract_fusion = (f32[2048,1024]{1,0:T(8,128)}, f32[2048,1024]{1,0:T(8,128)}) fusion(f32[2048,1024]{1,0:T(8,128)} %param.28, f32[2048,1024]{1,0:T(8,128)} %cotangent_ref.1, f32[1024,1024]{1,0:T(8,128)} %bitcast.226, f32[1024,1024]{1,0:T(8,128)} %bitcast.228, f32[2048]{0:T(1024)S(1)} %broadcast_multiply_fusion.2, f32[2048]{0:T(1024)S(1)} %copy-done.58, ...), kind=kLoop, calls=%fused_computation.3 | loop fusion | flops 18874368 | bytes 50360320 | tf_op jit(solution)/shard_map/sub | solution.py:1007
  (441 shorter events, 157.2 us)
Async XLA Ops:
  7.3 49.4 %all-gather.6.cloned.1.call-start = ((), (), s32[]{:S(2)}) async-start(), calls=%async_computation.3 | async-start | bytes 3538944 | tf_op jit(solution)/shard_map/all_gather | solution.py:809
  10.6 109.6 %all-gather.8.cloned.1.call-start = ((), (), s32[]{:S(2)}) async-start(), calls=%async_computation.8 | async-start | bytes 2506752 | tf_op jit(solution)/shard_map/all_gather | solution.py:32
  12.7 43.8 %collective-permute-start = (f32[16,1024]{1,0:T(8,128)S(1)}, f32[16,1024]{1,0:T(8,128)S(1)}, u32[]{:S(2)}, u32[]{:S(2)}) collective-permute-start(f32[16,1024]{1,0:T(8,128)S(1)} %slice_select_fusion), channel_id=1, source_target_pairs={{0,4},{4,8},{8,12},{12,16},{16,20},{20,24},{24,28},{1,5},{5,9},{9,... | collective-permute-start | bytes 196616 | tf_op jit(solution)/shard_map/ppermute | solution.py:26
  91.4 118.0 %all-gather.10.cloned.1.call-start = ((), (), s32[]{:S(2)}) async-start(), calls=%async_computation.9 | async-start | bytes 2506752 | tf_op jit(solution)/shard_map/all_gather | solution.py:32
  91.6 68.1 %copy-start.4 = (f32[1,512]{1,0:T(1,128)}, f32[1,512]{1,0:T(1,128)S(1)}, u32[]{:S(2)}) copy-start(f32[1,512]{1,0:T(1,128)S(1)} %broadcast_in_dim_reshape.3.skip_ref) | copy-start | bytes 6148
  175.5 94.5 %reduce-scatter.8.cloned.1.call-start = ((), (), s32[]{:S(2)}) async-start(), calls=%async_computation.7 | async-start | bytes 2359296 | tf_op jit(solution)/shard_map/reduce_scatter | solution.py:867
  195.7 170.6 %reduce-scatter.4.cloned.1.call-start = ((), (), s32[]{:S(2)}) async-start(), calls=%async_computation.4 | async-start | bytes 2621440 | tf_op jit(solution)/shard_map/reduce_scatter | solution.py:903
  209.0 85.4 %collective-permute-start.3 = (f16[528,1024]{1,0:T(8,128)(2,1)}, f16[528,1024]{1,0:T(8,128)(2,1)}, u32[]{:S(2)}, u32[]{:S(2)}) collective-permute-start(f16[528,1024]{1,0:T(8,128)(2,1)} %pad_maximum_fusion.3), channel_id=1, source_target_pairs={{0,1},{1,0},{2,3},{3,2},{4,5},{5,4},{6,7},{7,6},{8,9},{9,8},{10,11... | collective-permute-start | bytes 3244040 | tf_op jit(solution)/shard_map/ppermute | solution.py:72
  209.0 85.4 %collective-permute-start.5 = (f16[528,1024]{1,0:T(8,128)(2,1)}, f16[528,1024]{1,0:T(8,128)(2,1)}, u32[]{:S(2)}, u32[]{:S(2)}) collective-permute-start(f16[528,1024]{1,0:T(8,128)(2,1)} %pad_maximum_fusion.4), channel_id=1, source_target_pairs={{0,2},{1,3},{2,0},{3,1},{4,6},{5,7},{6,4},{7,5},{8,10},{9,11},{10,... | collective-permute-start | bytes 3244040 | tf_op jit(solution)/shard_map/ppermute | solution.py:72
  277.4 29.6 %collective-permute-start.1 = (f32[8,768]{1,0:T(8,128)S(1)}, f32[8,768]{1,0:T(8,128)S(1)}, u32[]{:S(2)}, u32[]{:S(2)}) collective-permute-start(f32[8,768]{1,0:T(8,128)S(1)} %slice_select_fusion.1), channel_id=1, source_target_pairs={{4,0},{8,4},{12,8},{16,12},{20,16},{24,20},{28,24},{5,1},{9,5},{13... | collective-permute-start | bytes 73736 | tf_op jit(solution)/shard_map/ppermute | solution.py:26
  301.5 79.7 %collective-permute-start.4 = (f16[272,1024]{1,0:T(8,128)(2,1)}, f16[272,1024]{1,0:T(8,128)(2,1)}, u32[]{:S(2)}, u32[]{:S(2)}) collective-permute-start(f16[272,1024]{1,0:T(8,128)(2,1)} %pad_maximum_fusion.6), channel_id=1, source_target_pairs={{0,2},{1,3},{2,0},{3,1},{4,6},{5,7},{6,4},{7,5},{8,10},{9,11},{10,... | collective-permute-start | bytes 1671176 | tf_op jit(solution)/shard_map/ppermute | solution.py:72
  304.9 80.5 %collective-permute-start.6 = (f16[272,1024]{1,0:T(8,128)(2,1)}, f16[272,1024]{1,0:T(8,128)(2,1)}, u32[]{:S(2)}, u32[]{:S(2)}) collective-permute-start(f16[272,1024]{1,0:T(8,128)(2,1)} %pad_maximum_fusion.7), channel_id=1, source_target_pairs={{0,1},{1,0},{2,3},{3,2},{4,5},{5,4},{6,7},{7,6},{8,9},{9,8},{10,11... | collective-permute-start | bytes 1671176 | tf_op jit(solution)/shard_map/ppermute | solution.py:72
  314.2 196.8 %reduce-scatter.6.cloned.1.call-start = ((), (), s32[]{:S(2)}) async-start(), calls=%async_computation.5 | async-start | bytes 6488064 | tf_op jit(solution)/shard_map/reduce_scatter | solution.py:960
  374.0 249.3 %all-reduce.9.cloned.1.call-start = ((), (), s32[]{:S(2)}) async-start(), calls=%async_computation.6 | async-start | bytes 294912 | tf_op jit(solution)/shard_map/psum | solution.py:985
  377.6 50.6 %collective-permute-start.8 = (f16[528,1024]{1,0:T(8,128)(2,1)S(1)}, f16[528,1024]{1,0:T(8,128)(2,1)S(1)}, u32[]{:S(2)}, u32[]{:S(2)}) collective-permute-start(f16[528,1024]{1,0:T(8,128)(2,1)S(1)} %pad_maximum_fusion.5), channel_id=1, source_target_pairs={{0,2},{1,3},{2,0},{3,1},{4,6},{5,7},{6,4},{7,5},{8,10},{9,11},{10,... | collective-permute-start | bytes 3244040 | tf_op jit(solution)/shard_map/ppermute | solution.py:72
  378.5 53.4 %collective-permute-start.2 = (f16[528,1024]{1,0:T(8,128)(2,1)S(1)}, f16[528,1024]{1,0:T(8,128)(2,1)S(1)}, u32[]{:S(2)}, u32[]{:S(2)}) collective-permute-start(f16[528,1024]{1,0:T(8,128)(2,1)S(1)} %pad_maximum_fusion.2), channel_id=1, source_target_pairs={{0,1},{1,0},{2,3},{3,2},{4,5},{5,4},{6,7},{7,6},{8,9},{9,8},{10,11... | collective-permute-start | bytes 3244040 | tf_op jit(solution)/shard_map/ppermute | solution.py:72
  385.4 83.4 %collective-permute-start.9 = (f16[1,272,1024]{2,1,0:T(8,128)(2,1)S(1)}, f16[1,272,1024]{2,1,0:T(8,128)(2,1)S(1)}, u32[]{:S(2)}, u32[]{:S(2)}) collective-permute-start(f16[1,272,1024]{2,1,0:T(8,128)(2,1)S(1)} %maximum_bitcast_fusion), channel_id=1, source_target_pairs={{0,2},{1,3},{2,0},{3,1},{4,6},{5,7},{6,4},{7,5},{8,10},{9,11},{10,... | collective-permute-start | bytes 1671176 | tf_op jit(solution)/shard_map/ppermute | solution.py:130
  389.9 75.0 %collective-permute-start.10 = (f16[1,272,1024]{2,1,0:T(8,128)(2,1)S(1)}, f16[1,272,1024]{2,1,0:T(8,128)(2,1)}, u32[]{:S(2)}, u32[]{:S(2)}) collective-permute-start(f16[1,272,1024]{2,1,0:T(8,128)(2,1)S(1)} %maximum_bitcast_fusion.1), channel_id=1, source_target_pairs={{0,1},{1,0},{2,3},{3,2},{4,5},{5,4},{6,7},{7,6},{8,9},{9,8},{10,11... | collective-permute-start | bytes 1671176 | tf_op jit(solution)/shard_map/ppermute | solution.py:130
  431.9 68.9 %collective-permute-start.12 = (f16[272,1024]{1,0:T(8,128)(2,1)}, f16[272,1024]{1,0:T(8,128)(2,1)S(1)}, u32[]{:S(2)}, u32[]{:S(2)}) collective-permute-start(f16[272,1024]{1,0:T(8,128)(2,1)} %pad_maximum_fusion.9), channel_id=1, source_target_pairs={{0,1},{1,0},{2,3},{3,2},{4,5},{5,4},{6,7},{7,6},{8,9},{9,8},{10,11... | collective-permute-start | bytes 1671176 | tf_op jit(solution)/shard_map/ppermute | solution.py:72
  436.0 64.8 %collective-permute-start.7 = (f16[272,1024]{1,0:T(8,128)(2,1)}, f16[272,1024]{1,0:T(8,128)(2,1)}, u32[]{:S(2)}, u32[]{:S(2)}) collective-permute-start(f16[272,1024]{1,0:T(8,128)(2,1)} %pad_maximum_fusion.8), channel_id=1, source_target_pairs={{0,2},{1,3},{2,0},{3,1},{4,6},{5,7},{6,4},{7,5},{8,10},{9,11},{10,... | collective-permute-start | bytes 1671176 | tf_op jit(solution)/shard_map/ppermute | solution.py:72
  468.8 89.0 %collective-permute-start.15 = (f16[2,272,1024]{2,1,0:T(8,128)(2,1)}, f16[2,272,1024]{2,1,0:T(8,128)(2,1)}, u32[]{:S(2)}, u32[]{:S(2)}) collective-permute-start(f16[2,272,1024]{2,1,0:T(8,128)(2,1)} %maximum_select_fusion.5), channel_id=1, source_target_pairs={{0,2},{1,3},{2,0},{3,1},{4,6},{5,7},{6,4},{7,5},{8,10},{9,11},{10,... | collective-permute-start | bytes 3342344 | tf_op jit(solution)/shard_map/ppermute | solution.py:130
  470.2 91.1 %collective-permute-start.14 = (f16[2,272,1024]{2,1,0:T(8,128)(2,1)}, f16[2,272,1024]{2,1,0:T(8,128)(2,1)}, u32[]{:S(2)}, u32[]{:S(2)}) collective-permute-start(f16[2,272,1024]{2,1,0:T(8,128)(2,1)} %maximum_select_fusion.4), channel_id=1, source_target_pairs={{0,1},{1,0},{2,3},{3,2},{4,5},{5,4},{6,7},{7,6},{8,9},{9,8},{10,11... | collective-permute-start | bytes 3342344 | tf_op jit(solution)/shard_map/ppermute | solution.py:130
  506.6 41.0 %collective-permute-start.13 = (f16[1,272,1024]{2,1,0:T(8,128)(2,1)S(1)}, f16[1,272,1024]{2,1,0:T(8,128)(2,1)S(1)}, u32[]{:S(2)}, u32[]{:S(2)}) collective-permute-start(f16[1,272,1024]{2,1,0:T(8,128)(2,1)S(1)} %maximum_bitcast_fusion.3), channel_id=1, source_target_pairs={{0,1},{1,0},{2,3},{3,2},{4,5},{5,4},{6,7},{7,6},{8,9},{9,8},{10,11... | collective-permute-start | bytes 1671176 | tf_op jit(solution)/shard_map/ppermute | solution.py:130
  508.4 40.7 %collective-permute-start.11 = (f16[1,272,1024]{2,1,0:T(8,128)(2,1)S(1)}, f16[1,272,1024]{2,1,0:T(8,128)(2,1)}, u32[]{:S(2)}, u32[]{:S(2)}) collective-permute-start(f16[1,272,1024]{2,1,0:T(8,128)(2,1)S(1)} %maximum_bitcast_fusion.2), channel_id=1, source_target_pairs={{0,2},{1,3},{2,0},{3,1},{4,6},{5,7},{6,4},{7,5},{8,10},{9,11},{10,... | collective-permute-start | bytes 1671176 | tf_op jit(solution)/shard_map/ppermute | solution.py:130
  552.0 75.8 %collective-permute-start.16 = (f16[2,272,1024]{2,1,0:T(8,128)(2,1)S(1)}, f16[2,272,1024]{2,1,0:T(8,128)(2,1)}, u32[]{:S(2)}, u32[]{:S(2)}) collective-permute-start(f16[2,272,1024]{2,1,0:T(8,128)(2,1)S(1)} %maximum_select_fusion.6), channel_id=1, source_target_pairs={{0,1},{1,0},{2,3},{3,2},{4,5},{5,4},{6,7},{7,6},{8,9},{9,8},{10,11... | collective-permute-start | bytes 3342344 | tf_op jit(solution)/shard_map/ppermute | solution.py:130
  552.1 78.4 %collective-permute-start.17 = (f16[2,272,1024]{2,1,0:T(8,128)(2,1)S(1)}, f16[2,272,1024]{2,1,0:T(8,128)(2,1)}, u32[]{:S(2)}, u32[]{:S(2)}) collective-permute-start(f16[2,272,1024]{2,1,0:T(8,128)(2,1)S(1)} %maximum_select_fusion.7), channel_id=1, source_target_pairs={{0,2},{1,3},{2,0},{3,1},{4,6},{5,7},{6,4},{7,5},{8,10},{9,11},{10,... | collective-permute-start | bytes 3342344 | tf_op jit(solution)/shard_map/ppermute | solution.py:130
  570.1 56.3 %copy-start.62 = (f32[5,2,32]{2,1,0:T(2,128)S(1)}, f32[5,2,32]{2,1,0:T(2,128)}, u32[]{:S(2)}) copy-start(f32[5,2,32]{2,1,0:T(2,128)} %param.36) | copy-start | bytes 3844
  570.1 56.3 %copy-start.70 = (f32[5,2,32]{2,1,0:T(2,128)S(1)}, f32[5,2,32]{2,1,0:T(2,128)}, u32[]{:S(2)}) copy-start(f32[5,2,32]{2,1,0:T(2,128)} %param.49) | copy-start | bytes 3844
  570.1 56.3 %copy-start.71 = (f32[5,2,32]{2,1,0:T(2,128)S(1)}, f32[5,2,32]{2,1,0:T(2,128)}, u32[]{:S(2)}) copy-start(f32[5,2,32]{2,1,0:T(2,128)} %param.50) | copy-start | bytes 3844
  570.1 57.0 %copy-start.53 = (f32[128,2,32]{0,2,1:T(8,128)S(1)}, f32[128,2,32]{0,2,1:T(8,128)}, u32[]{:S(2)}) copy-start(f32[128,2,32]{0,2,1:T(8,128)} %param.33) | copy-start | bytes 98308
  570.1 57.0 %copy-start.59 = (f32[128,2,32]{0,2,1:T(8,128)S(1)}, f32[128,2,32]{0,2,1:T(8,128)}, u32[]{:S(2)}) copy-start(f32[128,2,32]{0,2,1:T(8,128)} %param.43) | copy-start | bytes 98308
  570.1 57.0 %copy-start.60 = (f32[128,2,32]{0,2,1:T(8,128)S(1)}, f32[128,2,32]{0,2,1:T(8,128)}, u32[]{:S(2)}) copy-start(f32[128,2,32]{0,2,1:T(8,128)} %param.44) | copy-start | bytes 98308
  (80 other events, 854.7 us)
Sparse Core Ops, SparseCore 0:
  10.7 38.1 all-gather.5
  91.5 28.6 all-gather.7
  175.6 25.7 all-gather.9
  204.5 41.2 reduce-scatter.7
  314.3 51.8 reduce-scatter.3
  374.2 58.4 reduce-scatter.5
  557.8 65.4 all-reduce.8
